TPU v7x, 32 devices: a whole 2x2x4 slice. The times are simulated.
32 devices in a mesh: grp: 2 (over y), ctx: 4 (over z), head: 2 (over x), sub: 2 (over core).
Axes of the slice: x: 2, y: 2, z: 4, core: 2. Of those that a mesh axis runs over, the one named last changes fastest.
Arguments:
- queries: bfloat16 [1024, 8192], P(('grp', 'ctx'), 'head'), parts along dimension 0, may hold values from -120 to 120
- stretch_keys: bfloat16 [1024, 1024], P(('grp', 'ctx', 'sub'), 'head'), parts along dimension 0, may hold values from -6 to 6
- stretch_values: bfloat16 [1024, 1024], P(('grp', 'ctx', 'sub'), 'head'), parts along dimension 0, may hold values from -6 to 6
- cache_keys: bfloat16 [3072, 1024], P(('grp', 'ctx', 'sub'), 'head'), parts along dimension 0, may hold values from -6 to 6
- cache_values: bfloat16 [3072, 1024], P(('grp', 'ctx', 'sub'), 'head'), parts along dimension 0, may hold values from -6 to 6
- doc_lengths: int32 [24], P('grp'), parts along dimension 0, may hold values from 1 to 256, 2048 in all
Outputs:
- attended: bfloat16 [1024, 8192], P(('grp', 'ctx'), ('head', 'sub')), parts along dimension 0
There are 2 independent parts, one for each index of `grp`. A program takes and returns all parts, laid end to end along the dimension named above; each array names one. Nothing has to cross between parts.
Inputs may be any that keep to these rules, and one draw needn't show every extreme that they name: `doc_lengths`: the 12 documents fill all 2048 positions in order, none longer than 256 tokens and one exactly 256.
All inputs are finite; a program needn't handle non-finite values.
Results may differ from a plain program's by a relative error of at most 0.013.
Values may be sent and summed in bfloat16 or wider, within the bound.
No kernel may reach another device: no remote copies, remote signals or barrier semaphores. Data moves between devices by JAX's collectives and lax.ppermute only.
A program may use at most 64 MiB of HBM per device.

v0:
```python
import jax
import jax.numpy as jnp
from jax import lax
from jax.sharding import PartitionSpec as P

HEAD_DIM = 128


NEG_FILL = -1e30
FAR_POSITION = 1 << 30


def from_behind(x, axis, by):
    peers = lax.axis_size(axis)
    pairs = [(i, i + by) for i in range(peers) if 0 <= i + by < peers]
    return lax.ppermute(x, axis, pairs)


def shifted(value, axis, steps):
    count = lax.axis_size(axis)
    pairs = [(source, (source + steps) % count) for source in range(count)]
    return lax.ppermute(value, axis, pairs)


def joined(x, axis, combine):
    everything = jax.tree.map(
        lambda part, kind: lax.all_gather(part.astype(kind), axis),
        x,
        (jnp.bfloat16, jnp.bfloat16, jnp.bfloat16),
    )

    def take(k):
        return jax.tree.map(lambda part, own: part[k].astype(own.dtype), everything, x)

    return lax.fori_loop(
        1, lax.axis_size(axis), lambda k, so_far: combine(so_far, take(k)), take(0)
    )


def doc_number(positions, doc_ends):
    return jnp.sum((positions[:, None] >= doc_ends[None, :]).astype(jnp.int32), axis=1)


def join_partials(first, second):
    highest = jnp.maximum(first[0], second[0])
    first_scale = jnp.exp(first[0] - highest)
    second_scale = jnp.exp(second[0] - highest)
    return (
        highest,
        first[1] * first_scale + second[1] * second_scale,
        first[2] * first_scale[:, :, None] + second[2] * second_scale[:, :, None],
    )


def on_device(queries, stretch_keys, stretch_values, cache_keys, cache_values, doc_lengths):
    n_ctx = lax.axis_size("ctx")
    n_sub = lax.axis_size("sub")
    ctx_pos = lax.axis_index("ctx")
    sub_pos = lax.axis_index("sub")
    tok_rows = queries.shape[0]
    stretch_part = stretch_keys.shape[0]
    cache_part = cache_keys.shape[0]
    block_rows = stretch_part + cache_part
    prefix_len = cache_part * n_sub * n_ctx
    group_count = stretch_keys.shape[1] // HEAD_DIM
    per_group = queries.shape[1] // stretch_keys.shape[1]
    head_count = group_count * per_group
    score_scale = HEAD_DIM ** (-0.5)
    doc_ends = jnp.cumsum(doc_lengths)
    query_pos = prefix_len + ctx_pos * tok_rows + jnp.arange(tok_rows, dtype=jnp.int32)
    query_doc = doc_number(query_pos, doc_ends)
    query_heads = queries.reshape(tok_rows, group_count, per_group, HEAD_DIM)
    stacked = jnp.stack(
        [
            jnp.concatenate([stretch_keys, cache_keys], axis=0),
            jnp.concatenate([stretch_values, cache_values], axis=0),
        ]
    )

    def attend(partial_value, key_value, key_pos):
        key_doc = doc_number(key_pos, doc_ends)
        allowed = (key_doc[None, :] == query_doc[:, None]) & (
            key_pos[None, :] <= query_pos[:, None]
        )

        def compute(running):
            row_max, row_sum, weighted = running
            key_heads = key_value[0].reshape(-1, group_count, HEAD_DIM)
            value_heads = key_value[1].reshape(-1, group_count, HEAD_DIM)
            scores = jnp.einsum(
                "tgjd,kgd->gjtk", query_heads, key_heads, preferred_element_type=jnp.float32
            )
            scores = scores.reshape(head_count, tok_rows, -1) * score_scale
            scores = jnp.where(allowed[None], scores, NEG_FILL)
            new_max = jnp.maximum(row_max, jnp.max(scores, axis=2))
            shrink = jnp.exp(row_max - new_max)
            weights = jnp.where(allowed[None], jnp.exp(scores - new_max[:, :, None]), 0.0)
            row_sum = row_sum * shrink + jnp.sum(weights, axis=2)
            rounded = weights.astype(jnp.bfloat16).reshape(group_count, per_group, tok_rows, -1)
            update = jnp.einsum(
                "gjtk,kgd->gjtd", rounded, value_heads, preferred_element_type=jnp.float32
            )
            weighted = weighted * shrink[:, :, None] + update.reshape(
                head_count, tok_rows, HEAD_DIM
            )
            return (new_max, row_sum, weighted)

        return lax.cond(jnp.any(allowed), compute, lambda running: running, partial_value)

    initial = (
        jnp.full((head_count, tok_rows), NEG_FILL, jnp.float32),
        jnp.zeros((head_count, tok_rows), jnp.float32),
        jnp.zeros((head_count, tok_rows, HEAD_DIM), jnp.float32),
    )
    local_rows = jnp.arange(block_rows, dtype=jnp.int32)
    key_rows = ctx_pos * block_rows + local_rows
    shard_index = key_rows // block_rows
    within = key_rows % block_rows
    key_stretch_at = prefix_len + shard_index * tok_rows + sub_pos * stretch_part + within
    cache_at = shard_index * cache_part * n_sub + sub_pos * cache_part + within - stretch_part
    partial_value = attend(
        initial, stacked, jnp.where(within < stretch_part, key_stretch_at, cache_at)
    )
    stretch_pair = stacked[:, :stretch_part]
    stretch_within = jnp.arange(stretch_part, dtype=jnp.int32)
    for distance in range(1, n_ctx // 2 + 1):
        arrived = from_behind(stretch_pair, "ctx", distance)
        source = ctx_pos - distance
        stretch_at = prefix_len + source * tok_rows + sub_pos * stretch_part + stretch_within
        stretch_at = jnp.where(source >= 0, stretch_at, FAR_POSITION)
        partial_value = attend(partial_value, arrived, stretch_at)
        reach = (n_ctx // 2 + 1 - distance) * tok_rows
        tail_rows = min(cache_part, reach)
        tail_pair = stacked[:, block_rows - tail_rows :]
        tail_arrived = shifted(tail_pair, "ctx", distance)
        tail_source = (ctx_pos - distance) % n_ctx
        tail_at = (
            tail_source * cache_part * n_sub
            + sub_pos * cache_part
            + cache_part
            - tail_rows
            + jnp.arange(tail_rows, dtype=jnp.int32)
        )
        partial_value = attend(partial_value, tail_arrived, tail_at)
    row_max, row_sum, weighted = partial_value
    head_share = head_count // n_sub
    row_max, row_sum, weighted = joined((row_max, row_sum, weighted), "sub", join_partials)
    row_sum = lax.dynamic_slice_in_dim(row_sum, sub_pos * head_share, head_share, 0)
    weighted = lax.dynamic_slice_in_dim(weighted, sub_pos * head_share, head_share, 0)
    result = weighted / row_sum[:, :, None]
    return (
        jnp.transpose(result, (1, 0, 2))
        .reshape(tok_rows, head_share * HEAD_DIM)
        .astype(jnp.bfloat16)
    )


def solution(mesh):
    in_specs = (
        P(("grp", "ctx"), "head"),
        P(("grp", "ctx", "sub"), "head"),
        P(("grp", "ctx", "sub"), "head"),
        P(("grp", "ctx", "sub"), "head"),
        P(("grp", "ctx", "sub"), "head"),
        P("grp"),
    )
    out_specs = P(("grp", "ctx"), ("head", "sub"))
    return jax.shard_map(
        on_device, mesh=mesh, in_specs=in_specs, out_specs=out_specs, check_vma=False
    )
```

profile of v0, /device:TPU:15, one launch (start us, length us, event | category | flops | bytes accessed | tf_op | source)
XLA Modules:
  0.0 85.9 jit_solution(10614573850179915455)
XLA Ops:
  6.5 1.0 %copy.109 = bf16[64,512]{0,1:T(8,128)(2,1)S(1)} copy(bf16[64,512]{1,0:T(8,128)(2,1)} %param.17) | data formatting | bytes 131072 | tf_op args[1]
  7.5 1.0 %copy.112 = bf16[64,512]{0,1:T(8,128)(2,1)S(1)} copy(bf16[64,512]{1,0:T(8,128)(2,1)} %param.18) | data formatting | bytes 131072 | tf_op args[2]
  8.5 1.1 %copy.110 = bf16[192,512]{0,1:T(8,128)(2,1)S(1)} copy(bf16[192,512]{1,0:T(8,128)(2,1)} %param.19) | data formatting | bytes 393216 | tf_op args[3]
  9.5 1.1 %copy.113 = bf16[192,512]{0,1:T(8,128)(2,1)S(1)} copy(bf16[192,512]{1,0:T(8,128)(2,1)} %param.20) | data formatting | bytes 393216 | tf_op args[4]
  10.9 0.7 fusion.71
  11.7 4.9 %collective-permute-start.2 = (bf16[2,64,512]{1,2,0:T(8,128)(2,1)}, bf16[2,64,512]{1,2,0:T(8,128)(2,1)}, u32[]{:S(2)}, u32[]{:S(2)}) collective-permute-start(bf16[2,64,512]{1,2,0:T(8,128)(2,1)} %fusion.71), channel_id=1, source_target_pairs={{0,8},{4,12},{1,9},{5,13},{2,10},{6,14},{3,11},{7,15},{16,24},{20,... | collective-permute-start | bytes 393224 | tf_op jit(solution)/shard_map/ppermute | solution.py:16
  16.6 1.9 %collective-permute-start = (bf16[2,64,512]{1,2,0:T(8,128)(2,1)}, bf16[2,64,512]{1,2,0:T(8,128)(2,1)S(1)}, u32[]{:S(2)}, u32[]{:S(2)}) collective-permute-start(bf16[2,64,512]{1,2,0:T(8,128)(2,1)} %fusion.71), channel_id=1, source_target_pairs={{0,4},{4,8},{8,12},{1,5},{5,9},{9,13},{2,6},{6,10},{10,14},{3,7},{... | collective-permute-start | bytes 393224 | tf_op jit(solution)/shard_map/ppermute | solution.py:16
  18.5 0.7 pad_maximum_fusion
  19.3 1.0 %fusion.70 = bf16[2,192,512]{1,2,0:T(8,128)(2,1)} fusion(bf16[1,256,512]{1,2,0:T(8,128)(2,1)S(1)} %bitcast.126, bf16[1,256,512]{1,2,0:T(8,128)(2,1)S(1)} %bitcast.130), kind=kLoop, calls=%fused_computation.101 | loop fusion | flops 196608 | bytes 917504 | tf_op jit(solution)/shard_map/stack | solution.py:73
  20.3 2.6 %collective-permute-start.1 = (bf16[2,192,512]{1,2,0:T(8,128)(2,1)}, bf16[2,192,512]{1,2,0:T(8,128)(2,1)}, u32[]{:S(2)}, u32[]{:S(2)}) collective-permute-start(bf16[2,192,512]{1,2,0:T(8,128)(2,1)} %fusion.70), channel_id=1, source_target_pairs={{0,4},{4,8},{8,12},{12,0},{1,5},{5,9},{9,13},{13,1},{2,6},{6,10},{... | collective-permute-start | bytes 1179656 | tf_op jit(solution)/shard_map/ppermute | solution.py:22
  23.3 1.4 %fusion.80 = (pred[]{:T(512)}, pred[128,128]{0,1:T(8,128)(4,1)}) fusion(s32[128]{0:T(128)S(1)} %get-tuple-element.332, s32[128]{0:T(128)S(1)} %get-tuple-element.333, s32[128]{0:T(128)S(1)} %get-tuple-element.282, s32[128]{0:T(128)S(1)} %get-tuple-element.281), kind=kLoop, calls=%fused_computation.143 | loop fusion | flops 65535 | bytes 18433 | tf_op jit(solution)/shard_map/reduce_or | solution.py:108
  24.6 1.4 %fusion.78 = (pred[]{:T(512)}, pred[128,192]{0,1:T(8,128)(4,1)}) fusion(s32[128]{0:T(128)S(1)} %get-tuple-element.332, s32[192]{0:T(256)S(1)} %iota_add_fusion, s32[128]{0:T(128)S(1)} %get-tuple-element.282, s32[192]{0:T(256)S(1)} %convert_reduce_fusion.1), kind=kLoop, calls=%fused_computation.141 | loop fusion | flops 98303 | bytes 27137 | tf_op jit(solution)/shard_map/reduce_or | solution.py:108
  26.1 1.4 %fusion.77 = (pred[]{:T(512)}, pred[128,64]{0,1:T(8,128)(4,1)}, pred[]{:T(512)}, pred[128,64]{0,1:T(8,128)(4,1)}) fusion(s32[128]{0:T(128)S(1)} %get-tuple-element.332, s32[64]{0:T(128)S(1)} %get-tuple-element.334, s32[128]{0:T(128)S(1)} %get-tuple-element.282, s32[64]{0:T(128)S(1)} %get-tuple-element.279, s32[64]{0:T(128)S(1)} %get-tuple-element.335, ...), kind=kLoop, calls=%fused_computation.140 | loop fusion | flops 65534 | bytes 18434 | tf_op jit(solution)/shard_map/reduce_or | solution.py:108
  30.2 0.8 fusion.76
  32.4 5.3 %conditional.5 = (f32[32,128]{1,0:T(8,128)}, f32[32,128]{1,0:T(8,128)S(1)}, f32[32,128,128]{2,1,0:T(8,128)S(1)}) conditional(s32[]{:T(128)} %convert_element_type.134, () %tuple.39, (pred[128,256]{0,1:T(8,128)(4,1)S(1)}, bf16[256,512]{0,1:T(8,128)(2,1)S(1)}, bf16[128,4,8,128]{0,3,2,1:T(8,128)(2,1)S(1)}, bf16[256,512]{0,1:T(8,128)(2,1)S(1)}) %tuple.116), branch_computations={%region_12.13_spmd, %region_13.16_spmd} | conditional | flops 551047168 | bytes 20758552 | solution.py:108
  32.4 0.8 fusion
  33.2 1.1 %fusion.2 = f32[4,8,128]{2,1,0:T(8,128)S(1)} fusion(f32[4,256,128,8]{2,1,3,0:T(8,128)S(1)} %get-tuple-element.304, f32[4,8,128]{2,1,0:T(8,128)S(1)} %broadcast_maximum_fusion, pred[128,256]{0,1:T(8,128)(4,1)S(1)} %get-tuple-element.99), kind=kLoop, calls=%fused_computation.4 | loop fusion | flops 5238784 | bytes 4259840 | tf_op jit(solution)/shard_map/cond/branch_1_fun/reduce_sum | solution.py:98
  34.3 1.4 %fusion.3 = f32[4,8,128,128]{3,2,1,0:T(8,128)S(1)} fusion(bf16[256,4,128,1]{0,2,3,1:T(8,128)(2,1)S(1)} %bitcast.131, f32[4,256,128,8]{2,1,3,0:T(8,128)S(1)} %get-tuple-element.304, f32[4,8,128]{2,1,0:T(8,128)S(1)} %broadcast_maximum_fusion, pred[128,256]{0,1:T(8,128)(4,1)S(1)} %get-tuple-element.99), kind=kOutput, calls=%fused_computation.5 | convolution fusion | flops 273678336 | bytes 6602752 | tf_op jit(solution)/shard_map/cond/branch_1_fun/gjtk,kgd->gjtd/dot_general | solution.py:100
  37.0 0.7 bitcast_add_fusion.1
  37.7 1.3 %collective-permute-done = bf16[2,64,512]{1,2,0:T(8,128)(2,1)S(1)} collective-permute-done((bf16[2,64,512]{1,2,0:T(8,128)(2,1)}, bf16[2,64,512]{1,2,0:T(8,128)(2,1)S(1)}, u32[]{:S(2)}, u32[]{:S(2)}) %collective-permute-start) | collective-permute-done | bytes 131104 | tf_op jit(solution)/shard_map/ppermute | solution.py:16
  39.0 5.0 %conditional.6 = ((f32[32,128]{1,0:T(8,128)}, f32[32,128]{1,0:T(8,128)S(1)}, f32[32,128,128]{2,1,0:T(8,128)S(1)})) conditional(s32[]{:T(128)} %convert_element_type.132, (f32[32,128]{1,0:T(8,128)}, f32[32,128]{1,0:T(8,128)S(1)}, f32[32,128,128]{2,1,0:T(8,128)S(1)}) %conditional.5, (pred[128,64]{0,1:T(8,128)(4,1)}, ...), branch_computations={%region_16.17_spmd, %region_17.20_spmd} | conditional | flops 137633792 | bytes 13819964 | solution.py:108
  39.2 1.0 %fusion.82 = (f32[4,8,128]{2,1,0:T(8,128)S(1)}, f32[4,8,128,64]{2,3,1,0:T(8,128)S(1)}) fusion(bf16[128,4,8,128]{0,3,2,1:T(8,128)(2,1)S(1)} %get-tuple-element.257, bf16[64,4,128,1]{2,1,0,3:T(4,128)(2,1)S(1)} %bitcast.146, pred[128,64]{0,1:T(8,128)(4,1)} %get-tuple-element.112), kind=kOutput, calls=%fused_computation.145 | convolution fusion | flops 67891200 | bytes 2187264 | tf_op jit(solution)/shard_map/cond/branch_1_fun/tgjd,kgd->gjtk/dot_general | solution.py:90
  40.2 0.7 bitcast_maximum_fusion
  41.2 0.7 bitcast_add_fusion.3
  43.1 1.0 %bitcast_add_fusion.2 = f32[32,128,128]{2,1,0:T(8,128)S(1)} fusion(f32[4,8,128,128]{3,2,1,0:T(8,128)S(1)} %fusion.18, f32[32,128,128]{2,1,0:T(8,128)S(1)} %get-tuple-element.118, f32[32,128]{1,0:T(8,128)S(1)} %get-tuple-element.286), kind=kLoop, calls=%fused_computation.19 | loop fusion | flops 1048576 | bytes 6307840 | tf_op jit(solution)/shard_map/cond/branch_1_fun/add | solution.py:103
  44.1 11.8 %collective-permute-done.1 = bf16[2,192,512]{1,2,0:T(8,128)(2,1)} collective-permute-done((bf16[2,192,512]{1,2,0:T(8,128)(2,1)}, bf16[2,192,512]{1,2,0:T(8,128)(2,1)}, u32[]{:S(2)}, u32[]{:S(2)}) %collective-permute-start.1) | collective-permute-done | bytes 393248 | tf_op jit(solution)/shard_map/ppermute | solution.py:22
  56.6 1.1 %convert_element_type.135 = bf16[32,128,128]{2,1,0:T(8,128)(2,1)} convert(f32[32,128,128]{2,1,0:T(8,128)S(1)} %get-tuple-element.164) | non-fusion elementwise | flops 524288 | bytes 3145728 | tf_op jit(solution)/shard_map/convert_element_type | solution.py:27
  58.5 2.0 %all-gather.1 = bf16[64,128]{1,0:T(8,128)(2,1)S(1)} all-gather(bf16[32,128]{1,0:T(8,128)(2,1)S(1)} %convert_element_type.138), channel_id=3, replica_groups=mesh['grp'=2,'ctx'=4,'head'=2,'sub'=2] {'sub'}, dimensions={0}, use_global_device_ids=true | all-gather | bytes 24576 | tf_op jit(solution)/shard_map/all_gather | solution.py:27
  60.5 1.8 %all-gather.2 = bf16[64,128]{1,0:T(8,128)(2,1)S(1)} all-gather(bf16[32,128]{1,0:T(8,128)(2,1)S(1)} %convert_element_type.145), channel_id=4, replica_groups=mesh['grp'=2,'ctx'=4,'head'=2,'sub'=2] {'sub'}, dimensions={0}, use_global_device_ids=true | all-gather | bytes 24576 | tf_op jit(solution)/shard_map/all_gather | solution.py:27
  62.3 13.1 %all-gather.5.cloned.1.call-done = bf16[64,128,128]{2,1,0:T(8,128)(2,1)} async-done(((bf16[32,128,128]{2,1,0:T(8,128)(2,1)}), bf16[64,128,128]{2,1,0:T(8,128)(2,1)}) %all-gather.5.cloned.1.call-update) | async-done | bytes 2097168 | tf_op jit(solution)/shard_map/all_gather | solution.py:27
  75.4 1.7 %fusion.87 = (bf16[32,128,128]{2,1,0:T(8,128)(2,1)S(1)}, bf16[32,128,128]{2,1,0:T(8,128)(2,1)S(1)}) fusion(bf16[64,128,128]{2,1,0:T(8,128)(2,1)} %all-gather.5.cloned.1.call-done), kind=kLoop, calls=%fused_computation.150 | loop fusion | bytes 4194304 | tf_op jit(solution)/shard_map/slice | solution.py:33
  78.1 1.0 %copy.126 = bf16[128,2048]{1,0:T(8,128)(2,1)} copy(bf16[128,2048]{0,1:T(8,128)(2,1)S(1)} %bitcast.132) | data formatting | bytes 1048576 | tf_op jit(solution)/shard_map/convert_element_type | solution.py:154
  (47 shorter events, 6.7 us)
Async XLA Ops:
  6.5 68.9 %all-gather.5.cloned.1.call-start = ((), (), s32[]{:S(2)}) async-start(), calls=%async_computation | async-start | bytes 3145728 | tf_op jit(solution)/shard_map/all_gather | solution.py:27
  10.6 12.3 %copy-start.6 = (s32[12]{0:T(128)S(1)}, s32[12]{0:T(128)}, u32[]{:S(2)}) copy-start(s32[12]{0:T(128)} %param.21) | copy-start | bytes 148
  10.6 21.1 %copy-start = (bf16[128,4096]{1,0:T(8,128)(2,1)S(1)}, bf16[128,4096]{1,0:T(8,128)(2,1)}, u32[]{:S(2)}) copy-start(bf16[128,4096]{1,0:T(8,128)(2,1)} %param.16) | copy-start | bytes 3145732
  11.7 44.2 %collective-permute-start.2 = (bf16[2,64,512]{1,2,0:T(8,128)(2,1)}, bf16[2,64,512]{1,2,0:T(8,128)(2,1)}, u32[]{:S(2)}, u32[]{:S(2)}) collective-permute-start(bf16[2,64,512]{1,2,0:T(8,128)(2,1)} %fusion.71), channel_id=1, source_target_pairs={{0,8},{4,12},{1,9},{5,13},{2,10},{6,14},{3,11},{7,15},{16,24},{20,... | collective-permute-start | bytes 393224 | tf_op jit(solution)/shard_map/ppermute | solution.py:16
  16.6 22.4 %collective-permute-start = (bf16[2,64,512]{1,2,0:T(8,128)(2,1)}, bf16[2,64,512]{1,2,0:T(8,128)(2,1)S(1)}, u32[]{:S(2)}, u32[]{:S(2)}) collective-permute-start(bf16[2,64,512]{1,2,0:T(8,128)(2,1)} %fusion.71), channel_id=1, source_target_pairs={{0,4},{4,8},{8,12},{1,5},{5,9},{9,13},{2,6},{6,10},{10,14},{3,7},{... | collective-permute-start | bytes 393224 | tf_op jit(solution)/shard_map/ppermute | solution.py:16
  19.3 36.7 %collective-permute-start.3 = (bf16[2,128,512]{1,2,0:T(8,128)(2,1)}, bf16[2,128,512]{1,2,0:T(8,128)(2,1)}, u32[]{:S(2)}, u32[]{:S(2)}) collective-permute-start(bf16[2,128,512]{1,2,0:T(8,128)(2,1)} %pad_maximum_fusion), channel_id=1, source_target_pairs={{0,8},{4,12},{8,0},{12,4},{1,9},{5,13},{9,1},{13,5},{2,10},{6,14},... | collective-permute-start | bytes 786440 | tf_op jit(solution)/shard_map/ppermute | solution.py:22
  20.3 35.6 %collective-permute-start.1 = (bf16[2,192,512]{1,2,0:T(8,128)(2,1)}, bf16[2,192,512]{1,2,0:T(8,128)(2,1)}, u32[]{:S(2)}, u32[]{:S(2)}) collective-permute-start(bf16[2,192,512]{1,2,0:T(8,128)(2,1)} %fusion.70), channel_id=1, source_target_pairs={{0,4},{4,8},{8,12},{12,0},{1,5},{5,9},{9,13},{13,1},{2,6},{6,10},{... | collective-permute-start | bytes 1179656 | tf_op jit(solution)/shard_map/ppermute | solution.py:22
  39.1 1.8 %copy-start.5 = (pred[128,64]{0,1:T(8,128)(4,1)S(1)}, pred[128,64]{0,1:T(8,128)(4,1)}, u32[]{:S(2)}) copy-start(pred[128,64]{0,1:T(8,128)(4,1)} %get-tuple-element.112) | copy-start | bytes 24580 | tf_op jit(solution)/shard_map/cond
  55.9 0.7 copy-start.1
Sparse Core Ops, SparseCore 0:
  57.9 17.4 all-gather.4
where the time goes:
time: 86.3 us; the launch traced here: 85.9 us
  waiting for transfers between devices  26.2 us (30%)
  between operations  16.8 us (19%)
  other arithmetic  16.2 us (19%)
  local copies, waits for them, and re-layouts  9.58 us (11%)
  starting transfers between devices  9.49 us (11%)
  blocking collectives  3.77 us (4%)
  matrix products  3.76 us (4%)
    all_gather x1, waiting for transfers between devices, joined(): lax.all_gather(part.astype(kind), axis)  13.1 us
    ppermute x2, waiting for transfers between devices, shifted(): return lax.ppermute(value, axis, pairs)  11.8 us
    ppermute x2, starting transfers between devices, from_behind(): return lax.ppermute(x, axis, pairs)  6.84 us
    unnamed x13, local copies, waits for them, and re-layouts  5.98 us
    reduce_or x4, other arithmetic, attend(): jnp.any(allowed)  5.01 us
    all_gather x2, blocking collectives, joined(): lax.all_gather(part.astype(kind), axis)  3.77 us
    ppermute x2, starting transfers between devices, shifted(): return lax.ppermute(value, axis, pairs)  2.65 us
    another operation x3, other arithmetic, on_device(): jnp.stack([jnp.concatenate([stretch_keys, cache_keys], axis=0), jnp.conca...  2.48 us
  transfers between devices with their start and end apart: 5, of which 3 were waited for; matrix products, arithmetic and copies ran while one was open for 22% of the time, Pallas kernels for 0%

commit v1 on v0

v1 whole, which is shorter than its diff:
```python
import functools
import math

import jax
import jax.numpy as jnp
from jax import lax
from jax.experimental import pallas as pl
from jax.experimental.pallas import tpu as pltpu
from jax.sharding import PartitionSpec as P

HEAD_DIM = 128
NEG_FILL = -1e30
SCORE_SCALE = HEAD_DIM ** (-0.5)
EXP2_SCALE = SCORE_SCALE * math.log2(math.e)
DOT_HEADS = 4


def ring(x, axis, steps):
    count = lax.axis_size(axis)
    return lax.ppermute(x, axis, [(i, (i + steps) % count) for i in range(count)])


def window_kernel(
    reach, picks, prefix_len, place_ref, lengths_ref, q_ref, own_ref, *refs
):
    ring_refs, extra_refs, o_ref = refs[:reach], refs[reach:-1], refs[-1]
    tok_rows, head_cols = q_ref.shape
    kv_cols = own_ref.shape[-1] // 2
    group_count = kv_cols // HEAD_DIM
    per_group = head_cols // kv_cols
    ctx_pos = place_ref[0]
    first = prefix_len + ctx_pos * tok_rows

    own = own_ref[...].reshape(tok_rows, 2 * kv_cols)
    blocks = [own]
    for distance in range(1, reach + 1):
        block = ring_refs[distance - 1][...]
        for extra, dest in picks[distance]:
            block = jnp.where(ctx_pos == dest, extra_refs[extra][...], block)
        blocks.append(block)

    row = lax.broadcasted_iota(jnp.int32, (tok_rows, tok_rows), 0)
    lane = lax.broadcasted_iota(jnp.int32, (tok_rows, tok_rows), 1)
    doc_start = jnp.zeros((tok_rows, tok_rows), jnp.int32)
    end = jnp.int32(0)
    for doc in range(lengths_ref.shape[0]):
        end = end + lengths_ref[doc]
        doc_start = jnp.where(first + row >= end, end, doc_start)
    allowed = [(first + lane >= doc_start) & (lane <= row)]
    for distance in range(1, reach + 1):
        allowed.append(first - distance * tok_rows + lane >= doc_start)
    allowed = jnp.concatenate(allowed, axis=1)
    keys_len = allowed.shape[1]
    ones = jnp.ones((keys_len, HEAD_DIM), jnp.bfloat16)

    for group in range(group_count):
        at = group * HEAD_DIM
        keys = jnp.concatenate([b[:, at : at + HEAD_DIM] for b in blocks], axis=0)
        at = at + kv_cols
        values = jnp.concatenate([b[:, at : at + HEAD_DIM] for b in blocks], axis=0)
        values = jnp.concatenate([values, ones], axis=1)
        for head in range(group * per_group, (group + 1) * per_group):
            here = pl.ds(head * HEAD_DIM, HEAD_DIM)
            scores = lax.dot_general(
                q_ref[:, here],
                keys,
                (((1,), (1,)), ((), ())),
                preferred_element_type=jnp.float32,
            )
            scores = jnp.where(allowed, scores, NEG_FILL)
            row_max = jnp.max(scores, axis=1, keepdims=True)
            rounded = jnp.exp2((scores - row_max) * EXP2_SCALE).astype(jnp.bfloat16)
            summed = jnp.dot(rounded, values, preferred_element_type=jnp.float32)
            o_ref[:, here] = (summed[:, :HEAD_DIM] / summed[:, HEAD_DIM:]).astype(o_ref.dtype)


def plan_extras(n_ctx, reach, per_shard):
    rounds = []
    for back in range(2, reach + 1):
        source = n_ctx - 1 - (back - 1) // per_shard
        block = per_shard - 1 - (back - 1) % per_shard
        for dest in range(reach + 1 - back):
            for step in rounds:
                if source not in step and all(d != dest for _, d, _ in step.values()):
                    break
            else:
                step = {}
                rounds.append(step)
            step[source] = (block, dest, dest + back)
    return rounds


def on_device(queries, stretch_keys, stretch_values, cache_keys, cache_values, doc_lengths):
    n_ctx = lax.axis_size("ctx")
    n_sub = lax.axis_size("sub")
    ctx_pos = lax.axis_index("ctx")
    sub_pos = lax.axis_index("sub")
    tok_rows = queries.shape[0]
    stretch_part = stretch_keys.shape[0]
    cache_part = cache_keys.shape[0]
    prefix_len = cache_part * n_sub * n_ctx
    group_count = stretch_keys.shape[1] // HEAD_DIM
    head_cols = queries.shape[1] // n_sub
    reach = n_ctx // 2
    per_shard = cache_part * n_sub // tok_rows

    keys = jnp.concatenate([stretch_keys, cache_keys], axis=0)
    values = jnp.concatenate([stretch_values, cache_values], axis=0)
    if group_count % n_sub == 0:
        kv_cols = stretch_keys.shape[1] // n_sub

        def share(which):
            at = which * kv_cols
            return jnp.concatenate(
                [
                    lax.dynamic_slice_in_dim(keys, at, kv_cols, 1),
                    lax.dynamic_slice_in_dim(values, at, kv_cols, 1),
                ],
                axis=1,
            )

        mine = share(sub_pos)
        theirs = share(1 - sub_pos)
    else:
        mine = theirs = jnp.concatenate([keys, values], axis=1)
    peers = lax.ppermute(theirs, "sub", [(0, 1), (1, 0)])
    halves = jnp.where(sub_pos == 0, jnp.stack([mine, peers]), jnp.stack([peers, mine]))
    own = halves[:, :stretch_part].reshape(tok_rows, -1)
    cached = halves[:, stretch_part:].reshape(n_sub * cache_part, -1)

    def cached_block(block):
        return lax.dynamic_slice_in_dim(cached, block * tok_rows, tok_rows, 0)

    outgoing = jnp.where(ctx_pos == n_ctx - 1, cached_block(per_shard - 1), own)
    rings = [ring(outgoing, "ctx", distance) for distance in range(1, reach + 1)]
    extras, picks = [], [[] for _ in range(reach + 1)]
    for step in plan_extras(n_ctx, reach, per_shard):
        blocks = [step.get(source, (0,))[0] for source in range(n_ctx)]
        block = jnp.take(jnp.array(blocks, jnp.int32), ctx_pos)
        if len(step) == 1:
            block = max(blocks)
        pairs = [(source, dest) for source, (_, dest, _) in step.items()]
        for _, dest, slot in step.values():
            picks[slot].append((len(extras), dest))
        extras.append(lax.ppermute(cached_block(block), "ctx", pairs))

    mine_q = lax.dynamic_slice_in_dim(queries, sub_pos * head_cols, head_cols, 1)
    vmem = pl.BlockSpec(memory_space=pltpu.VMEM)
    smem = pl.BlockSpec(memory_space=pltpu.SMEM)
    return pl.pallas_call(
        functools.partial(window_kernel, reach, picks, prefix_len),
        out_shape=jax.ShapeDtypeStruct((tok_rows, head_cols), queries.dtype),
        in_specs=[smem, smem] + [vmem] * (2 + reach + len(extras)),
        out_specs=vmem,
        compiler_params=pltpu.CompilerParams(vmem_limit_bytes=24 << 20),
    )(ctx_pos[None], doc_lengths, mine_q, own, *rings, *extras)


def solution(mesh):
    in_specs = (
        P(("grp", "ctx"), "head"),
        P(("grp", "ctx", "sub"), "head"),
        P(("grp", "ctx", "sub"), "head"),
        P(("grp", "ctx", "sub"), "head"),
        P(("grp", "ctx", "sub"), "head"),
        P("grp"),
    )
    out_specs = P(("grp", "ctx"), ("head", "sub"))
    return jax.shard_map(
        on_device, mesh=mesh, in_specs=in_specs, out_specs=out_specs, check_vma=False
    )
```

time: 86.3 us -> 24.7 us (0.29)
  the two profiles are of different devices: /device:TPU:15 before, /device:TPU:0 now
where the time goes in v1:
time: 24.7 us; the launch traced here: 24.5 us
  waiting for transfers between devices  10.4 us (42%)
  starting transfers between devices  7.4 us (30%)
  local copies, waits for them, and re-layouts  3.51 us (14%)
  Pallas kernels  2.94 us (12%)
    ppermute x1, waiting for transfers between devices, on_device(): extras.append(lax.ppermute(cached_block(block), 'ctx', pairs))  7.65 us
    ppermute x2, starting transfers between devices, ring(): lax.ppermute(x, axis, [(i, (i + steps) % count) for i in range(count)])  5.6 us
    unnamed x10, local copies, waits for them, and re-layouts  3.35 us
    pallas_call x1, Pallas kernels, on_device(): pl.pallas_call(functools.partial(window_kernel, reach, picks, prefix_len)...  2.94 us
    ppermute x2, waiting for transfers between devices, ring(): lax.ppermute(x, axis, [(i, (i + steps) % count) for i in range(count)])  1.65 us
    ppermute x1, starting transfers between devices, on_device(): extras.append(lax.ppermute(cached_block(block), 'ctx', pairs))  1.28 us
    ppermute x1, waiting for transfers between devices, on_device(): peers = lax.ppermute(theirs, 'sub', [(0, 1), (1, 0)])  1.14 us
    ppermute x1, starting transfers between devices, on_device(): peers = lax.ppermute(theirs, 'sub', [(0, 1), (1, 0)])  0.52 us
  transfers between devices with their start and end apart: 4, of which 3 were waited for; matrix products, arithmetic and copies ran while one was open for 0% of the time, Pallas kernels for 0%

profile of v1, /device:TPU:0, one launch (start us, length us, event | category | flops | bytes accessed | tf_op | source)
XLA Modules:
  0.0 24.5 jit_solution(13010080419936990982)
XLA Ops:
  0.0 0.0 copy-start
  0.0 0.0 copy-start.2
  0.0 0.9 %constant_dynamic-update-slice_fusion.1 = bf16[256,512]{1,0:T(8,128)(2,1)S(1)} fusion(bf16[64,512]{1,0:T(8,128)(2,1)} %param.7), kind=kLoop, calls=%fused_computation.5 | loop fusion | bytes 131072
  0.9 0.8 %constant_dynamic-update-slice_fusion.3 = bf16[256,512]{1,0:T(8,128)(2,1)S(1)} fusion(bf16[64,512]{1,0:T(8,128)(2,1)} %param.8), kind=kLoop, calls=%fused_computation.7 | loop fusion | bytes 131072
  1.8 0.0 copy-done.2
  1.8 0.0 copy-start.3
  1.8 0.9 %copy-done.3 = bf16[192,512]{1,0:T(8,128)(2,1)S(1)} copy-done((bf16[192,512]{1,0:T(8,128)(2,1)S(1)}, bf16[192,512]{1,0:T(8,128)(2,1)}, u32[]{:S(2)}) %copy-start.3) | copy-done | bytes 196632
  2.8 0.5 %collective-permute-start = (bf16[256,512]{1,0:T(8,128)(2,1)S(1)}, bf16[256,512]{1,0:T(8,128)(2,1)S(1)}, u32[]{:S(2)}, u32[]{:S(2)}) collective-permute-start(bf16[256,512]{1,0:T(8,128)(2,1)S(1)} %pad_maximum_fusion), channel_id=1, source_target_pairs={{0,1},{1,0},{2,3},{3,2},{4,5},{5,4},{6,7},{7,6},{8,9},{9,8},{10,11... | collective-permute-start | bytes 786440 | tf_op jit(solution)/shard_map/ppermute | solution.py:126
  3.4 1.1 %collective-permute-done = bf16[256,512]{1,0:T(8,128)(2,1)S(1)} collective-permute-done((bf16[256,512]{1,0:T(8,128)(2,1)S(1)}, bf16[256,512]{1,0:T(8,128)(2,1)S(1)}, u32[]{:S(2)}, u32[]{:S(2)}) %collective-permute-start) | collective-permute-done | bytes 262176 | tf_op jit(solution)/shard_map/ppermute | solution.py:126
  4.5 0.1 maximum_select_fusion
  4.7 4.0 %collective-permute-start.2 = (bf16[128,512]{1,0:T(8,128)(2,1)S(1)}, bf16[128,512]{1,0:T(8,128)(2,1)S(1)}, u32[]{:S(2)}, u32[]{:S(2)}) collective-permute-start(bf16[128,512]{1,0:T(8,128)(2,1)S(1)} %get-tuple-element.6), channel_id=1, source_target_pairs={{0,8},{4,12},{8,0},{12,4},{1,9},{5,13},{9,1},{13,5},{2,10},{6,14},... | collective-permute-start | bytes 393224 | tf_op jit(solution)/shard_map/ppermute | solution.py:20
  8.7 1.6 %collective-permute-start.1 = (bf16[128,512]{1,0:T(8,128)(2,1)S(1)}, bf16[128,512]{1,0:T(8,128)(2,1)S(1)}, u32[]{:S(2)}, u32[]{:S(2)}) collective-permute-start(bf16[128,512]{1,0:T(8,128)(2,1)S(1)} %get-tuple-element.6), channel_id=1, source_target_pairs={{0,4},{4,8},{8,12},{12,0},{1,5},{5,9},{9,13},{13,1},{2,6},{6,10},{... | collective-permute-start | bytes 393224 | tf_op jit(solution)/shard_map/ppermute | solution.py:20
  10.3 1.3 %collective-permute-start.3 = (bf16[128,512]{1,0:T(8,128)(2,1)S(1)}, bf16[128,512]{1,0:T(8,128)(2,1)S(1)}, u32[]{:S(2)}, u32[]{:S(2)}) collective-permute-start(bf16[128,512]{1,0:T(8,128)(2,1)S(1)} %get-tuple-element.5), channel_id=1, source_target_pairs={{12,0},{13,1},{14,2},{15,3},{28,16},{29,17},{30,18},{31,19}} | collective-permute-start | bytes 393224 | tf_op jit(solution)/shard_map/ppermute | solution.py:145
  11.6 0.0 copy-done
  11.6 7.7 %collective-permute-done.3.refs_2_ = bf16[128,512]{1,0:T(8,128)(2,1)S(1)} collective-permute-done((bf16[128,512]{1,0:T(8,128)(2,1)S(1)}, bf16[128,512]{1,0:T(8,128)(2,1)S(1)}, u32[]{:S(2)}, u32[]{:S(2)}) %collective-permute-start.3) | collective-permute-done | bytes 131104 | tf_op jit(solution)/shard_map/ppermute | solution.py:145
  19.3 1.6 %collective-permute-done.2.refs_1_ = bf16[128,512]{1,0:T(8,128)(2,1)S(1)} collective-permute-done((bf16[128,512]{1,0:T(8,128)(2,1)S(1)}, bf16[128,512]{1,0:T(8,128)(2,1)S(1)}, u32[]{:S(2)}, u32[]{:S(2)}) %collective-permute-start.2) | collective-permute-done | bytes 131104 | tf_op jit(solution)/shard_map/ppermute | solution.py:20
  20.9 0.0 collective-permute-done.1.refs_0_
  20.9 0.0 copy-start.1
  20.9 0.7 %copy-done.1 = s32[12]{0:T(128)S(1)} copy-done((s32[12]{0:T(128)S(1)}, s32[12]{0:T(128)}, u32[]{:S(2)}) %copy-start.1) | copy-done | bytes 72
  21.6 2.9 %shard_map.64 = bf16[128,2048]{1,0:T(8,128)(2,1)} custom-call(s32[1]{0:T(128)} %bitcast.place_ref, s32[12]{0:T(128)S(1)} %copy-done.1, bf16[128,2048]{1,0:T(8,128)(2,1)S(1)} %constant_dynamic-slice_fusion.4.q_ref, bf16[128,512]{1,0:T(8,128)(2,1)S(1)} %bitcast.7, bf16[128,512]{1,0:T(8,128)(2,1)S(1)} %collective-permute-done.1.refs_0_, ...), custom_call_target="tpu_custom_call" | custom-call | tf_op jit(solution)/shard_map/pallas_call | solution.py:150
  (9 shorter events, 0.2 us)
Async XLA Ops:
  0.0 11.6 %copy-start = (bf16[128,4096]{1,0:T(8,128)(2,1)S(1)}, bf16[128,4096]{1,0:T(8,128)(2,1)}, u32[]{:S(2)}) copy-start(bf16[128,4096]{1,0:T(8,128)(2,1)} %param.6) | copy-start | bytes 3145732
  0.0 1.8 %copy-start.2 = (bf16[192,512]{1,0:T(8,128)(2,1)S(1)}, bf16[192,512]{1,0:T(8,128)(2,1)}, u32[]{:S(2)}) copy-start(bf16[192,512]{1,0:T(8,128)(2,1)} %param.9) | copy-start | bytes 589828
  1.8 0.9 %copy-start.3 = (bf16[192,512]{1,0:T(8,128)(2,1)S(1)}, bf16[192,512]{1,0:T(8,128)(2,1)}, u32[]{:S(2)}) copy-start(bf16[192,512]{1,0:T(8,128)(2,1)} %param.10) | copy-start | bytes 589828
  2.8 1.7 %collective-permute-start = (bf16[256,512]{1,0:T(8,128)(2,1)S(1)}, bf16[256,512]{1,0:T(8,128)(2,1)S(1)}, u32[]{:S(2)}, u32[]{:S(2)}) collective-permute-start(bf16[256,512]{1,0:T(8,128)(2,1)S(1)} %pad_maximum_fusion), channel_id=1, source_target_pairs={{0,1},{1,0},{2,3},{3,2},{4,5},{5,4},{6,7},{7,6},{8,9},{9,8},{10,11... | collective-permute-start | bytes 786440 | tf_op jit(solution)/shard_map/ppermute | solution.py:126
  4.7 16.2 %collective-permute-start.2 = (bf16[128,512]{1,0:T(8,128)(2,1)S(1)}, bf16[128,512]{1,0:T(8,128)(2,1)S(1)}, u32[]{:S(2)}, u32[]{:S(2)}) collective-permute-start(bf16[128,512]{1,0:T(8,128)(2,1)S(1)} %get-tuple-element.6), channel_id=1, source_target_pairs={{0,8},{4,12},{8,0},{12,4},{1,9},{5,13},{9,1},{13,5},{2,10},{6,14},... | collective-permute-start | bytes 393224 | tf_op jit(solution)/shard_map/ppermute | solution.py:20
  8.7 12.2 %collective-permute-start.1 = (bf16[128,512]{1,0:T(8,128)(2,1)S(1)}, bf16[128,512]{1,0:T(8,128)(2,1)S(1)}, u32[]{:S(2)}, u32[]{:S(2)}) collective-permute-start(bf16[128,512]{1,0:T(8,128)(2,1)S(1)} %get-tuple-element.6), channel_id=1, source_target_pairs={{0,4},{4,8},{8,12},{12,0},{1,5},{5,9},{9,13},{13,1},{2,6},{6,10},{... | collective-permute-start | bytes 393224 | tf_op jit(solution)/shard_map/ppermute | solution.py:20
  10.3 9.0 %collective-permute-start.3 = (bf16[128,512]{1,0:T(8,128)(2,1)S(1)}, bf16[128,512]{1,0:T(8,128)(2,1)S(1)}, u32[]{:S(2)}, u32[]{:S(2)}) collective-permute-start(bf16[128,512]{1,0:T(8,128)(2,1)S(1)} %get-tuple-element.5), channel_id=1, source_target_pairs={{12,0},{13,1},{14,2},{15,3},{28,16},{29,17},{30,18},{31,19}} | collective-permute-start | bytes 393224 | tf_op jit(solution)/shard_map/ppermute | solution.py:145
  20.9 0.7 %copy-start.1 = (s32[12]{0:T(128)S(1)}, s32[12]{0:T(128)}, u32[]{:S(2)}) copy-start(s32[12]{0:T(128)} %lengths_ref.1) | copy-start | bytes 148

commit v2 on v1

v2 whole, which is shorter than its diff:
```python
import functools
import math

import jax
import jax.numpy as jnp
from jax import lax
from jax.experimental import pallas as pl
from jax.experimental.pallas import tpu as pltpu
from jax.sharding import PartitionSpec as P

HEAD_DIM = 128
NEG_FILL = -1e30
SCORE_SCALE = HEAD_DIM ** (-0.5)
EXP2_SCALE = SCORE_SCALE * math.log2(math.e)


def ring(x, axis, steps):
    count = lax.axis_size(axis)
    return lax.ppermute(x, axis, [(i, (i + steps) % count) for i in range(count)])


def pack_kernel(tok_rows, n_ctx, prefix_len, k_ref, v_ref, ck_ref, cv_ref, len_ref,
                mine_ref, theirs_ref, branch_ref, bias_ref, lengths, sems, len_sem):
    sub_pos = lax.axis_index("sub")
    stretch_part, cache_part = k_ref.shape[0], ck_ref.shape[0]
    kv_cols = mine_ref.shape[1] // 2
    split = kv_cols != k_ref.shape[1]
    copies = [pltpu.make_async_copy(len_ref, lengths, len_sem)]
    for out, owner in enumerate([sub_pos, 1 - sub_pos]):
        dst = (mine_ref, theirs_ref)[out]
        at = pl.multiple_of(owner * kv_cols, HEAD_DIM) if split else 0
        for i, (src, row, rows, col) in enumerate([
            (k_ref, 0, stretch_part, 0),
            (v_ref, 0, stretch_part, kv_cols),
            (ck_ref, stretch_part, cache_part, 0),
            (cv_ref, stretch_part, cache_part, kv_cols),
        ]):
            copies.append(
                pltpu.make_async_copy(
                    src.at[:, pl.ds(at, kv_cols)],
                    dst.at[pl.ds(row, rows), pl.ds(col, kv_cols)],
                    sems.at[out, i],
                )
            )
    for copy in copies:
        copy.start()
    copies[0].wait()
    starts = [jnp.int32(0)] * n_ctx
    end = jnp.int32(0)
    for doc in range(lengths.shape[0]):
        end = end + lengths[doc]
        for c in range(n_ctx):
            starts[c] = jnp.where(end <= prefix_len + c * tok_rows, end, starts[c])
    beyond = [prefix_len + c * tok_rows - starts[c] > tok_rows for c in range(n_ctx)]
    any_beyond = functools.reduce(jnp.logical_or, beyond)
    branch_ref[0] = jnp.where(beyond[0], 2, jnp.where(any_beyond, 1, 0))
    write_bias(prefix_len + lax.axis_index("ctx") * tok_rows, lengths, bias_ref)
    for copy in copies[1:]:
        copy.wait()


def write_bias(first, lengths, bias_ref):
    tok_rows = bias_ref.shape[0]
    row = lax.broadcasted_iota(jnp.int32, (tok_rows, tok_rows), 0)
    lane = lax.broadcasted_iota(jnp.int32, (tok_rows, tok_rows), 1)
    doc_start = jnp.zeros((tok_rows, tok_rows), jnp.int32)
    end = jnp.int32(0)
    for doc in range(lengths.shape[0]):
        end = end + lengths[doc]
        doc_start = jnp.where(first + row >= end, end, doc_start)
    for distance in range(bias_ref.shape[1] // tok_rows):
        allowed = first - distance * tok_rows + lane >= doc_start
        if distance == 0:
            allowed = allowed & (lane <= row)
        bias_ref[:, distance * tok_rows : (distance + 1) * tok_rows] = jnp.where(
            allowed, 0.0, NEG_FILL
        )


def window_kernel(picks, q_ref, bias_ref, *refs):
    own_ref, before_ref, *later_refs, o_ref = refs
    ctx_pos = lax.axis_index("ctx")
    blocks = [own_ref[...], before_ref[...]] + [None] * (bias_ref.shape[1] // q_ref.shape[0] - 2)
    for later_ref, pick in zip(later_refs, picks):
        for slot in sorted({slot for _, slot in pick}):
            here = [ctx_pos == dest for dest, at in pick if at == slot]
            block = later_ref[...]
            if blocks[slot] is not None:
                block = jnp.where(functools.reduce(jnp.logical_or, here), block, blocks[slot])
            blocks[slot] = block
    kv_cols = own_ref.shape[-1] // 2
    group_count = kv_cols // HEAD_DIM
    per_group = q_ref.shape[1] // kv_cols
    ones = jnp.ones((bias_ref.shape[1], HEAD_DIM), jnp.bfloat16)
    for group in range(group_count):
        at = group * HEAD_DIM
        keys = jnp.concatenate([b[:, at : at + HEAD_DIM] for b in blocks], axis=0)
        at = at + kv_cols
        values = jnp.concatenate([b[:, at : at + HEAD_DIM] for b in blocks], axis=0)
        values = jnp.concatenate([values, ones], axis=1)
        for head in range(group * per_group, (group + 1) * per_group):
            here = pl.ds(head * HEAD_DIM, HEAD_DIM)
            scores = lax.dot_general(
                q_ref[:, here],
                keys,
                (((1,), (1,)), ((), ())),
                preferred_element_type=jnp.float32,
            )
            scores = scores + bias_ref[...]
            row_max = jnp.max(scores, axis=1, keepdims=True)
            rounded = jnp.exp2((scores - row_max) * EXP2_SCALE).astype(jnp.bfloat16)
            summed = jnp.dot(rounded, values, preferred_element_type=jnp.float32)
            o_ref[:, here] = (summed[:, :HEAD_DIM] / summed[:, HEAD_DIM:]).astype(o_ref.dtype)


def plan_rounds(n_ctx, reach, per_shard):
    wanted = []
    for dest in range(n_ctx):
        for slot in range(2, reach + 1):
            back = slot - dest
            if back <= 0:
                wanted.append((dest - slot, 0, dest, slot))
            else:
                source = n_ctx - 1 - (back - 1) // per_shard
                wanted.append((source, per_shard - (back - 1) % per_shard, dest, slot))
    rounds = []
    for source, block, dest, slot in wanted:
        for step in rounds:
            if source not in step and all(d != dest for _, d, _ in step.values()):
                break
        else:
            step = {}
            rounds.append(step)
        step[source] = (block, dest, slot)
    return rounds


def on_device(queries, stretch_keys, stretch_values, cache_keys, cache_values, doc_lengths):
    n_ctx = lax.axis_size("ctx")
    n_sub = lax.axis_size("sub")
    ctx_pos = lax.axis_index("ctx")
    sub_pos = lax.axis_index("sub")
    tok_rows = queries.shape[0]
    stretch_part = stretch_keys.shape[0]
    cache_part = cache_keys.shape[0]
    part_rows = stretch_part + cache_part
    prefix_len = cache_part * n_sub * n_ctx
    group_count = stretch_keys.shape[1] // HEAD_DIM
    head_cols = queries.shape[1] // n_sub
    reach = n_ctx // 2
    per_shard = cache_part * n_sub // tok_rows
    kv_cols = stretch_keys.shape[1]
    if group_count % n_sub == 0:
        kv_cols = kv_cols // n_sub
    vmem = pl.BlockSpec(memory_space=pltpu.VMEM)
    smem = pl.BlockSpec(memory_space=pltpu.SMEM)
    hbm = pl.BlockSpec(memory_space=pltpu.HBM)

    half = jax.ShapeDtypeStruct((part_rows, 2 * kv_cols), stretch_keys.dtype)
    allowed = jax.ShapeDtypeStruct((tok_rows, (reach + 1) * tok_rows), jnp.float32)
    mine, theirs, branch, bias = pl.pallas_call(
        functools.partial(pack_kernel, tok_rows, n_ctx, prefix_len),
        out_shape=[half, half, jax.ShapeDtypeStruct((1,), jnp.int32), allowed],
        in_specs=[hbm] * 5,
        out_specs=[vmem, vmem, smem, vmem],
        scratch_shapes=[
            pltpu.SMEM(doc_lengths.shape, jnp.int32),
            pltpu.SemaphoreType.DMA((2, 4)),
            pltpu.SemaphoreType.DMA,
        ],
        compiler_params=pltpu.CompilerParams(vmem_limit_bytes=8 << 20),
    )(
        *[
            pltpu.with_memory_space_constraint(x, pltpu.HBM)
            for x in (stretch_keys, stretch_values, cache_keys, cache_values, doc_lengths)
        ]
    )
    peers = lax.ppermute(theirs, "sub", [(0, 1), (1, 0)])
    halves = jnp.where(sub_pos == 0, jnp.stack([mine, peers]), jnp.stack([peers, mine]))
    blocks = jnp.concatenate(
        [
            halves[:, :stretch_part].reshape(tok_rows, -1),
            halves[:, stretch_part:].reshape(n_sub * cache_part, -1),
        ]
    )
    own = blocks[:tok_rows]

    def block_at(index):
        return lax.dynamic_slice_in_dim(blocks, index * tok_rows, tok_rows, 0)

    outgoing = block_at(jnp.where(ctx_pos == n_ctx - 1, per_shard, 0))
    later, picks = [], []
    for step in plan_rounds(n_ctx, reach, per_shard):
        which = max(block for block, _, _ in step.values())
        for source, (block, _, _) in step.items():
            which = jnp.where(ctx_pos == source, block, which)
        pairs = [(source, dest) for source, (_, dest, _) in step.items()]
        later.append(lax.ppermute(block_at(which), "ctx", pairs))
        picks.append([(dest, slot) for _, dest, slot in step.values()])
    before = ring(outgoing, "ctx", 1)

    mine_q = lax.dynamic_slice_in_dim(queries, sub_pos * head_cols, head_cols, 1)
    return pl.pallas_call(
        functools.partial(window_kernel, picks),
        out_shape=jax.ShapeDtypeStruct((tok_rows, head_cols), queries.dtype),
        in_specs=[vmem] * (4 + len(later)),
        out_specs=vmem,
        compiler_params=pltpu.CompilerParams(vmem_limit_bytes=24 << 20),
    )(mine_q, bias, own, before, *later)


def solution(mesh):
    in_specs = (
        P(("grp", "ctx"), "head"),
        P(("grp", "ctx", "sub"), "head"),
        P(("grp", "ctx", "sub"), "head"),
        P(("grp", "ctx", "sub"), "head"),
        P(("grp", "ctx", "sub"), "head"),
        P("grp"),
    )
    out_specs = P(("grp", "ctx"), ("head", "sub"))
    return jax.shard_map(
        on_device, mesh=mesh, in_specs=in_specs, out_specs=out_specs, check_vma=False
    )
```

time: 24.7 us -> 19.1 us (0.77)
  the two profiles are of different devices: /device:TPU:0 before, /device:TPU:12 now
where the time goes in v2:
time: 19.1 us; the launch traced here: 18.9 us
  waiting for transfers between devices  7.99 us (42%)
  starting transfers between devices  6.13 us (32%)
  Pallas kernels  4.15 us (22%)
  other arithmetic  0.44 us (2%)
    ppermute x2, waiting for transfers between devices, on_device(): later.append(lax.ppermute(block_at(which), 'ctx', pairs))  6.48 us
    ppermute x2, starting transfers between devices, on_device(): later.append(lax.ppermute(block_at(which), 'ctx', pairs))  4.43 us
    pallas_call x1, Pallas kernels, on_device(): pl.pallas_call(functools.partial(window_kernel, picks), out_shape=jax.Sha...  2.36 us
    pallas_call x1, Pallas kernels, on_device(): pl.pallas_call(functools.partial(pack_kernel, tok_rows, n_ctx, prefix_len...  1.78 us
    ppermute x1, starting transfers between devices, ring(): lax.ppermute(x, axis, [(i, (i + steps) % count) for i in range(count)])  1.63 us
    ppermute x1, waiting for transfers between devices, on_device(): peers = lax.ppermute(theirs, 'sub', [(0, 1), (1, 0)])  1.5 us
  transfers between devices with their start and end apart: 4, of which 3 were waited for; matrix products, arithmetic and copies ran while one was open for 0% of the time, Pallas kernels for 0%

profile of v2, /device:TPU:12, one launch (start us, length us, event | category | flops | bytes accessed | tf_op | source)
XLA Modules:
  0.0 18.9 jit_solution(4900680614639471692)
XLA Ops:
  0.0 0.0 copy-start
  0.0 1.8 %shard_map.64 = (bf16[256,512]{1,0:T(8,128)(2,1)S(1)}, bf16[256,512]{1,0:T(8,128)(2,1)S(1)}, s32[1]{0:T(128)}, f32[128,384]{1,0:T(8,128)S(1)}) custom-call(bf16[64,512]{1,0:T(8,128)(2,1)} %k_ref.1, bf16[64,512]{1,0:T(8,128)(2,1)} %v_ref.1, bf16[192,512]{1,0:T(8,128)(2,1)} %ck_ref.1, bf16[192,512]{1,0:T(8,128)(2,1)} %cv_ref.1, s32[12]{0:T(128)} %len_ref.1), custom_call_target="tpu_custom_call" | custom-call | tf_op jit(solution)/shard_map/pallas_call | solution.py:161
  1.8 0.1 collective-permute-start
  1.9 1.5 %collective-permute-done = bf16[256,512]{1,0:T(8,128)(2,1)S(1)} collective-permute-done((bf16[256,512]{1,0:T(8,128)(2,1)S(1)}, bf16[256,512]{1,0:T(8,128)(2,1)S(1)}, u32[]{:S(2)}, u32[]{:S(2)}) %collective-permute-start) | collective-permute-done | bytes 262176 | tf_op jit(solution)/shard_map/ppermute | solution.py:178
  3.4 0.1 maximum_select_fusion
  3.5 0.4 %fusion = (bf16[128,512]{1,0:T(8,128)(2,1)S(1)}, bf16[128,512]{1,0:T(8,128)(2,1)S(1)}, bf16[128,512]{1,0:T(8,128)(2,1)S(1)}) fusion(s32[]{:T(128)S(6)} %select_n.38, bf16[384,512]{1,0:T(8,128)(2,1)S(1)} %bitcast.7, bf16[128,512]{1,0:T(8,128)(2,1)S(1)} %bitcast.4, s32[]{:T(128)S(6)} %select_n.35), kind=kLoop, calls=%fused_computation.5 | loop fusion | flops 524288 | bytes 1048584 | tf_op jit(solution)/shard_map/concatenate | solution.py:180
  3.9 1.6 %collective-permute-start.1 = (bf16[128,512]{1,0:T(8,128)(2,1)S(1)}, bf16[128,512]{1,0:T(8,128)(2,1)S(1)}, u32[]{:S(2)}, u32[]{:S(2)}) collective-permute-start(bf16[128,512]{1,0:T(8,128)(2,1)S(1)} %get-tuple-element.12), channel_id=1, source_target_pairs={{0,4},{4,8},{8,12},{12,0},{1,5},{5,9},{9,13},{13,1},{2,6},{6,10},{... | collective-permute-start | bytes 393224 | tf_op jit(solution)/shard_map/ppermute | solution.py:19
  5.5 3.1 %collective-permute-start.2 = (bf16[128,512]{1,0:T(8,128)(2,1)S(1)}, bf16[128,512]{1,0:T(8,128)(2,1)S(1)}, u32[]{:S(2)}, u32[]{:S(2)}) collective-permute-start(bf16[128,512]{1,0:T(8,128)(2,1)S(1)} %get-tuple-element.11), channel_id=1, source_target_pairs={{12,0},{0,8},{4,12},{13,1},{1,9},{5,13},{14,2},{2,10},{6,14},{15,3... | collective-permute-start | bytes 393224 | tf_op jit(solution)/shard_map/ppermute | solution.py:198
  8.7 1.3 %collective-permute-start.3 = (bf16[128,512]{1,0:T(8,128)(2,1)S(1)}, bf16[128,512]{1,0:T(8,128)(2,1)S(1)}, u32[]{:S(2)}, u32[]{:S(2)}) collective-permute-start(bf16[128,512]{1,0:T(8,128)(2,1)S(1)} %get-tuple-element.13), channel_id=1, source_target_pairs={{12,4},{13,5},{14,6},{15,7},{28,20},{29,21},{30,22},{31,23}} | collective-permute-start | bytes 393224 | tf_op jit(solution)/shard_map/ppermute | solution.py:198
  10.0 0.0 copy-done
  10.0 0.0 collective-permute-done.1.refs_1_
  10.0 4.3 %collective-permute-done.2.refs_2_ = bf16[128,512]{1,0:T(8,128)(2,1)S(1)} collective-permute-done((bf16[128,512]{1,0:T(8,128)(2,1)S(1)}, bf16[128,512]{1,0:T(8,128)(2,1)S(1)}, u32[]{:S(2)}, u32[]{:S(2)}) %collective-permute-start.2) | collective-permute-done | bytes 131104 | tf_op jit(solution)/shard_map/ppermute | solution.py:198
  14.3 2.2 %collective-permute-done.3.refs_3_ = bf16[128,512]{1,0:T(8,128)(2,1)S(1)} collective-permute-done((bf16[128,512]{1,0:T(8,128)(2,1)S(1)}, bf16[128,512]{1,0:T(8,128)(2,1)S(1)}, u32[]{:S(2)}, u32[]{:S(2)}) %collective-permute-start.3) | collective-permute-done | bytes 131104 | tf_op jit(solution)/shard_map/ppermute | solution.py:198
  16.5 2.4 %shard_map.65 = bf16[128,2048]{1,0:T(8,128)(2,1)} custom-call(bf16[128,2048]{1,0:T(8,128)(2,1)S(1)} %constant_dynamic-slice_fusion.q_ref, f32[128,384]{1,0:T(8,128)S(1)} %get-tuple-element.8.bias_ref, bf16[128,512]{1,0:T(8,128)(2,1)S(1)} %bitcast.5, bf16[128,512]{1,0:T(8,128)(2,1)S(1)} %collective-permute-done.1.refs_1_, ...), custom_call_target="tpu_custom_call" | custom-call | tf_op jit(solution)/shard_map/pallas_call | solution.py:203
  (3 shorter events, 0.1 us)
Async XLA Ops:
  0.0 10.0 %copy-start = (bf16[128,4096]{1,0:T(8,128)(2,1)S(1)}, bf16[128,4096]{1,0:T(8,128)(2,1)}, u32[]{:S(2)}) copy-start(bf16[128,4096]{1,0:T(8,128)(2,1)} %param.6) | copy-start | bytes 3145732
  1.8 1.6 %collective-permute-start = (bf16[256,512]{1,0:T(8,128)(2,1)S(1)}, bf16[256,512]{1,0:T(8,128)(2,1)S(1)}, u32[]{:S(2)}, u32[]{:S(2)}) collective-permute-start(bf16[256,512]{1,0:T(8,128)(2,1)S(1)} %get-tuple-element.10), channel_id=1, source_target_pairs={{0,1},{1,0},{2,3},{3,2},{4,5},{5,4},{6,7},{7,6},{8,9},{9,8},{10,11... | collective-permute-start | bytes 786440 | tf_op jit(solution)/shard_map/ppermute | solution.py:178
  3.9 6.1 %collective-permute-start.1 = (bf16[128,512]{1,0:T(8,128)(2,1)S(1)}, bf16[128,512]{1,0:T(8,128)(2,1)S(1)}, u32[]{:S(2)}, u32[]{:S(2)}) collective-permute-start(bf16[128,512]{1,0:T(8,128)(2,1)S(1)} %get-tuple-element.12), channel_id=1, source_target_pairs={{0,4},{4,8},{8,12},{12,0},{1,5},{5,9},{9,13},{13,1},{2,6},{6,10},{... | collective-permute-start | bytes 393224 | tf_op jit(solution)/shard_map/ppermute | solution.py:19
  5.5 8.8 %collective-permute-start.2 = (bf16[128,512]{1,0:T(8,128)(2,1)S(1)}, bf16[128,512]{1,0:T(8,128)(2,1)S(1)}, u32[]{:S(2)}, u32[]{:S(2)}) collective-permute-start(bf16[128,512]{1,0:T(8,128)(2,1)S(1)} %get-tuple-element.11), channel_id=1, source_target_pairs={{12,0},{0,8},{4,12},{13,1},{1,9},{5,13},{14,2},{2,10},{6,14},{15,3... | collective-permute-start | bytes 393224 | tf_op jit(solution)/shard_map/ppermute | solution.py:198
  8.7 7.9 %collective-permute-start.3 = (bf16[128,512]{1,0:T(8,128)(2,1)S(1)}, bf16[128,512]{1,0:T(8,128)(2,1)S(1)}, u32[]{:S(2)}, u32[]{:S(2)}) collective-permute-start(bf16[128,512]{1,0:T(8,128)(2,1)S(1)} %get-tuple-element.13), channel_id=1, source_target_pairs={{12,4},{13,5},{14,6},{15,7},{28,20},{29,21},{30,22},{31,23}} | collective-permute-start | bytes 393224 | tf_op jit(solution)/shard_map/ppermute | solution.py:198

commit v3 on v2

v3 whole, which is shorter than its diff:
```python
import functools
import math

import jax
import jax.numpy as jnp
from jax import lax
from jax.experimental import pallas as pl
from jax.experimental.pallas import tpu as pltpu
from jax.sharding import PartitionSpec as P

HEAD_DIM = 128
NEG_FILL = -1e30
SCORE_SCALE = HEAD_DIM ** (-0.5)
EXP2_SCALE = SCORE_SCALE * math.log2(math.e)


def swap_cores(x):
    return lax.ppermute(x, "sub", [(0, 1), (1, 0)])


def pack_kernel(n_ctx, k_ref, v_ref, ck_ref, cv_ref, raw_ref, mine_ref, theirs_ref, sems):
    sub_pos = lax.axis_index("sub")
    last = lax.axis_index("ctx") == n_ctx - 1
    stretch_part, all_cols = k_ref.shape
    cache_part = ck_ref.shape[0]
    kv_cols = mine_ref.shape[1] // 2
    split = kv_cols != all_cols
    copies = []
    for i, (own_src, cache_src) in enumerate([(k_ref, ck_ref), (v_ref, cv_ref)]):
        dst = raw_ref.at[:, pl.ds(i * all_cols, all_cols)]
        from_own = pltpu.make_async_copy(own_src, dst, sems.at[0, i])
        tail = cache_src.at[pl.ds(cache_part - stretch_part, stretch_part), :]
        from_cache = pltpu.make_async_copy(tail, dst, sems.at[0, i])
        pl.when(last)(from_cache.start)
        pl.when(jnp.logical_not(last))(from_own.start)
        copies.append(from_own)
    for out, owner in ((2, 1 - sub_pos), (1, sub_pos)):
        dst = (None, mine_ref, theirs_ref)[out]
        at = pl.multiple_of(owner * kv_cols, HEAD_DIM) if split else 0
        for i, (src, row, rows, col) in enumerate([
            (k_ref, 0, stretch_part, 0),
            (v_ref, 0, stretch_part, kv_cols),
            (ck_ref, stretch_part, cache_part, 0),
            (cv_ref, stretch_part, cache_part, kv_cols),
        ]):
            copy = pltpu.make_async_copy(
                src.at[:, pl.ds(at, kv_cols)],
                dst.at[pl.ds(row, rows), pl.ds(col, kv_cols)],
                sems.at[out, i],
            )
            copy.start()
            copies.append(copy)
    for copy in copies:
        copy.wait()


def bias_kernel(prefix_len, stretch_part, cache_part, len_ref, bias_ref, lengths, sem):
    copy = pltpu.make_async_copy(len_ref, lengths, sem)
    copy.start()
    sub_pos, ctx_pos = lax.axis_index("sub"), lax.axis_index("ctx")
    tok_rows = bias_ref.shape[0]
    n_sub = tok_rows // stretch_part
    first = prefix_len + ctx_pos * tok_rows
    row = lax.broadcasted_iota(jnp.int32, (tok_rows, tok_rows), 0)
    lane = lax.broadcasted_iota(jnp.int32, (tok_rows, tok_rows), 1)
    doc_start = jnp.zeros((tok_rows, tok_rows), jnp.int32)
    copy.wait()
    end = jnp.int32(0)
    for doc in range(lengths.shape[0]):
        end = end + lengths[doc]
        doc_start = jnp.where(first + row >= end, end, doc_start)
    for slot in range(bias_ref.shape[1] // tok_rows):
        at = first - slot * tok_rows
        low, high = at + sub_pos * stretch_part, at + (1 - sub_pos) * stretch_part
        if slot == 1:
            tail = prefix_len - (n_sub - 1) * cache_part - stretch_part
            low = jnp.where(ctx_pos == 0, tail + sub_pos * cache_part, low)
            high = jnp.where(ctx_pos == 0, tail + (1 - sub_pos) * cache_part, high)
        elif slot > 1:
            at = jnp.where(ctx_pos == 0, prefix_len - cache_part, at) if slot == 2 else at
            low = jnp.where(ctx_pos < slot, at, low)
            high = jnp.where(ctx_pos < slot, at + stretch_part, high)
        key = jnp.where(lane < stretch_part, low + lane, high + lane - stretch_part)
        allowed = key >= doc_start
        if slot == 0:
            allowed = allowed & (key <= first + row)
        bias_ref[:, slot * tok_rows : (slot + 1) * tok_rows] = jnp.where(allowed, 0.0, NEG_FILL)


def window_kernel(picks, q_ref, bias_ref, own_ref, peer_ref, near_ref, far_ref, *refs):
    later_refs, o_ref = refs[:-1], refs[-1]
    ctx_pos = lax.axis_index("ctx")
    stretch_part, kv_cols = near_ref.shape[0], own_ref.shape[1] // 2
    own = own_ref[:stretch_part], peer_ref[:stretch_part]
    all_cols = near_ref.shape[1] // 2
    at = [0, all_cols]
    if all_cols != kv_cols:
        at = [pl.multiple_of(lax.axis_index("sub") * kv_cols + x, HEAD_DIM) for x in at]
    near = jnp.concatenate([near_ref[:, pl.ds(x, kv_cols)] for x in at], axis=1)
    blocks = [jnp.concatenate(own, axis=0), jnp.concatenate([near, far_ref[...]], axis=0)]
    blocks += [None] * (bias_ref.shape[1] // q_ref.shape[0] - 2)
    for later_ref, pick in zip(later_refs, picks):
        for slot in sorted({slot for _, slot in pick}):
            here = [ctx_pos == dest for dest, at in pick if at == slot]
            block = later_ref[...]
            if blocks[slot] is not None:
                block = jnp.where(functools.reduce(jnp.logical_or, here), block, blocks[slot])
            blocks[slot] = block
    group_count = kv_cols // HEAD_DIM
    per_group = q_ref.shape[1] // kv_cols
    ones = jnp.ones((bias_ref.shape[1], HEAD_DIM), jnp.bfloat16)
    for group in range(group_count):
        at = group * HEAD_DIM
        keys = jnp.concatenate([b[:, at : at + HEAD_DIM] for b in blocks], axis=0)
        at = at + kv_cols
        values = jnp.concatenate([b[:, at : at + HEAD_DIM] for b in blocks], axis=0)
        values = jnp.concatenate([values, ones], axis=1)
        for head in range(group * per_group, (group + 1) * per_group):
            here = pl.ds(head * HEAD_DIM, HEAD_DIM)
            scores = lax.dot_general(
                q_ref[:, here],
                keys,
                (((1,), (1,)), ((), ())),
                preferred_element_type=jnp.float32,
            )
            scores = scores + bias_ref[...]
            row_max = jnp.max(scores, axis=1, keepdims=True)
            rounded = jnp.exp2((scores - row_max) * EXP2_SCALE).astype(jnp.bfloat16)
            summed = jnp.dot(rounded, values, preferred_element_type=jnp.float32)
            o_ref[:, here] = (summed[:, :HEAD_DIM] / summed[:, HEAD_DIM:]).astype(o_ref.dtype)


def plan_rounds(n_ctx, reach, tok_rows, cache_part, shard_rows):
    per_shard = shard_rows // tok_rows
    cached, stretch = [], []
    for dest in range(n_ctx):
        for slot in range(2, reach + 1):
            back = slot - dest
            if back <= 0:
                stretch.append((dest - slot, None, dest, slot))
                continue
            source = n_ctx - 1 - (back - 1) // per_shard
            row = shard_rows - ((back - 1) % per_shard + 1) * tok_rows
            if dest == 0 and back == 2:
                row = cache_part
            cached.append((source, row, dest, slot))
    rounds = []
    for source, row, dest, slot in cached + stretch:
        dests = [{d for _, d, _ in step.values()} for step in rounds]
        free = [i for i, step in enumerate(rounds) if source not in step and dest not in dests[i]]
        free.sort(key=lambda i: source not in dests[i])
        if not free:
            rounds.append({})
            free = [len(rounds) - 1]
        rounds[free[0]][source] = (row, dest, slot)
    return rounds


def on_device(queries, stretch_keys, stretch_values, cache_keys, cache_values, doc_lengths):
    n_ctx = lax.axis_size("ctx")
    n_sub = lax.axis_size("sub")
    ctx_pos = lax.axis_index("ctx")
    sub_pos = lax.axis_index("sub")
    tok_rows = queries.shape[0]
    stretch_part, all_cols = stretch_keys.shape
    cache_part = cache_keys.shape[0]
    prefix_len = cache_part * n_sub * n_ctx
    head_cols = queries.shape[1] // n_sub
    reach = n_ctx // 2
    assert cache_part == 3 * stretch_part and tok_rows == 2 * stretch_part
    kv_cols = all_cols // n_sub if all_cols // HEAD_DIM % n_sub == 0 else all_cols
    vmem = pl.BlockSpec(memory_space=pltpu.VMEM)
    hbm = pl.BlockSpec(memory_space=pltpu.HBM)
    small = pltpu.CompilerParams(vmem_limit_bytes=8 << 20)

    def in_hbm(*arrays):
        return [pltpu.with_memory_space_constraint(x, pltpu.HBM) for x in arrays]

    half = jax.ShapeDtypeStruct((stretch_part + cache_part, 2 * kv_cols), stretch_keys.dtype)
    raw, mine, theirs = pl.pallas_call(
        functools.partial(pack_kernel, n_ctx),
        out_shape=[
            jax.ShapeDtypeStruct((stretch_part, 2 * all_cols), stretch_keys.dtype), half, half
        ],
        in_specs=[hbm] * 4,
        out_specs=[vmem] * 3,
        scratch_shapes=[pltpu.SemaphoreType.DMA((3, 4))],
        compiler_params=small,
    )(*in_hbm(stretch_keys, stretch_values, cache_keys, cache_values))
    bias = pl.pallas_call(
        functools.partial(bias_kernel, prefix_len, stretch_part, cache_part),
        out_shape=jax.ShapeDtypeStruct((tok_rows, (reach + 1) * tok_rows), jnp.float32),
        in_specs=[hbm],
        out_specs=vmem,
        scratch_shapes=[pltpu.SMEM(doc_lengths.shape, jnp.int32), pltpu.SemaphoreType.DMA],
        compiler_params=small,
    )(*in_hbm(doc_lengths))

    peers = swap_cores(theirs)
    near = lax.ppermute(raw, "ctx", [(i, (i + 1) % n_ctx) for i in range(n_ctx)])

    def cached_rows(row):
        parts = []
        for owner in range(n_sub):
            low = max(row, owner * cache_part) - owner * cache_part + stretch_part
            high = min(row + tok_rows, (owner + 1) * cache_part) - owner * cache_part + stretch_part
            if low < high:
                parts.append(jnp.where(sub_pos == owner, mine[low:high], peers[low:high]))
        return jnp.concatenate(parts) if len(parts) > 1 else parts[0]

    own = jnp.concatenate([mine[:stretch_part], peers[:stretch_part]])
    sent, later, picks = [], [], []
    for step in plan_rounds(n_ctx, reach, tok_rows, cache_part, cache_part * n_sub):
        block = own
        for source, (row, _, _) in step.items():
            if row is not None:
                block = jnp.where(ctx_pos == source, cached_rows(row), block)
        pairs = [(source, dest) for source, (_, dest, _) in step.items()]
        sent.append(block)
        later.append(lax.ppermute(block, "ctx", pairs))
        picks.append([(dest, slot) for _, dest, slot in step.values()])

    near, *_ = lax.optimization_barrier((near, *sent[::-1]))
    if kv_cols != all_cols:
        at = (1 - sub_pos) * kv_cols
        near_theirs = jnp.concatenate(
            [
                lax.dynamic_slice_in_dim(near, at, kv_cols, 1),
                lax.dynamic_slice_in_dim(near, at + all_cols, kv_cols, 1),
            ],
            axis=1,
        )
    else:
        near_theirs = near
    far = swap_cores(near_theirs)
    mine_q = lax.dynamic_slice_in_dim(queries, sub_pos * head_cols, head_cols, 1)
    return pl.pallas_call(
        functools.partial(window_kernel, picks),
        out_shape=jax.ShapeDtypeStruct((tok_rows, head_cols), queries.dtype),
        in_specs=[vmem] * (6 + len(later)),
        out_specs=vmem,
        compiler_params=pltpu.CompilerParams(vmem_limit_bytes=24 << 20),
    )(mine_q, bias, mine, peers, near, far, *later)


def solution(mesh):
    in_specs = (
        P(("grp", "ctx"), "head"),
        P(("grp", "ctx", "sub"), "head"),
        P(("grp", "ctx", "sub"), "head"),
        P(("grp", "ctx", "sub"), "head"),
        P(("grp", "ctx", "sub"), "head"),
        P("grp"),
    )
    out_specs = P(("grp", "ctx"), ("head", "sub"))
    return jax.shard_map(
        on_device, mesh=mesh, in_specs=in_specs, out_specs=out_specs, check_vma=False
    )
```

time: 19.1 us -> 17.2 us (0.901)
  the two profiles are of different devices: /device:TPU:12 before, /device:TPU:0 now
where the time goes in v3:
time: 17.2 us; the launch traced here: 17 us
  starting transfers between devices  8.39 us (49%)
  Pallas kernels  4.45 us (26%)
  waiting for transfers between devices  3.93 us (23%)
    ppermute x2, starting transfers between devices, on_device(): later.append(lax.ppermute(block, 'ctx', pairs))  5.17 us
    ppermute x2, waiting for transfers between devices, on_device(): later.append(lax.ppermute(block, 'ctx', pairs))  2.67 us
    ppermute x1, starting transfers between devices, on_device(): lax.ppermute(raw, 'ctx', [(i, (i + 1) % n_ctx) for i in range(n_ctx)])  2.64 us
    pallas_call x1, Pallas kernels, on_device(): pl.pallas_call(functools.partial(window_kernel, picks), out_shape=jax.Sha...  2.35 us
    pallas_call x1, Pallas kernels, on_device(): pl.pallas_call(functools.partial(pack_kernel, n_ctx), out_shape=[jax.Shap...  1.35 us
    ppermute x1, waiting for transfers between devices, on_device(): lax.ppermute(raw, 'ctx', [(i, (i + 1) % n_ctx) for i in range(n_ctx)])  0.83 us
    pallas_call x1, Pallas kernels, on_device(): pl.pallas_call(functools.partial(bias_kernel, prefix_len, stretch_part, c...  0.75 us
    ppermute x2, starting transfers between devices, swap_cores(): return lax.ppermute(x, 'sub', [(0, 1), (1, 0)])  0.59 us
  transfers between devices with their start and end apart: 5, of which 3 were waited for; matrix products, arithmetic and copies ran while one was open for 1% of the time, Pallas kernels for 4%

profile of v3, /device:TPU:0, one launch (start us, length us, event | category | flops | bytes accessed | tf_op | source)
XLA Modules:
  0.0 17.0 jit_solution(14933370915820397858)
XLA Ops:
  0.0 0.0 copy-start
  0.0 1.4 %shard_map.65 = (bf16[64,1024]{1,0:T(8,128)(2,1)S(1)}, bf16[256,512]{1,0:T(8,128)(2,1)S(1)}, bf16[256,512]{1,0:T(8,128)(2,1)S(1)}) custom-call(bf16[64,512]{1,0:T(8,128)(2,1)} %k_ref.1, bf16[64,512]{1,0:T(8,128)(2,1)} %v_ref.1, bf16[192,512]{1,0:T(8,128)(2,1)} %ck_ref.1, bf16[192,512]{1,0:T(8,128)(2,1)} %cv_ref.1), custom_call_target="tpu_custom_call" | custom-call | tf_op jit(solution)/shard_map/pallas_call | solution.py:180
  1.4 0.5 %collective-permute-start = (bf16[256,512]{1,0:T(8,128)(2,1)S(1)}, bf16[256,512]{1,0:T(8,128)(2,1)S(1)}, u32[]{:S(2)}, u32[]{:S(2)}) collective-permute-start(bf16[256,512]{1,0:T(8,128)(2,1)S(1)} %get-tuple-element.10), channel_id=1, source_target_pairs={{0,1},{1,0},{2,3},{3,2},{4,5},{5,4},{6,7},{7,6},{8,9},{9,8},{10,11... | collective-permute-start | bytes 786440 | tf_op jit(solution)/shard_map/ppermute | solution.py:18
  1.9 2.6 %collective-permute-start.1 = (bf16[64,1024]{1,0:T(8,128)(2,1)S(1)}, bf16[64,1024]{1,0:T(8,128)(2,1)S(1)}, u32[]{:S(2)}, u32[]{:S(2)}) collective-permute-start(bf16[64,1024]{1,0:T(8,128)(2,1)S(1)} %get-tuple-element.11), channel_id=1, source_target_pairs={{0,4},{4,8},{8,12},{12,0},{1,5},{5,9},{9,13},{13,1},{2,6},{6,10},{... | collective-permute-start | bytes 393224 | tf_op jit(solution)/shard_map/ppermute | solution.py:200
  4.5 0.0 collective-permute-done.peer_ref
  4.5 0.1 fusion
  4.6 4.5 %collective-permute-start.3 = (bf16[128,512]{1,0:T(8,128)(2,1)S(1)}, bf16[128,512]{1,0:T(8,128)(2,1)S(1)}, u32[]{:S(2)}, u32[]{:S(2)}) collective-permute-start(bf16[128,512]{1,0:T(8,128)(2,1)S(1)} %get-tuple-element.13), channel_id=1, source_target_pairs={{12,0},{0,8},{13,1},{1,9},{14,2},{2,10},{15,3},{3,11},{28,16},{16,... | collective-permute-start | bytes 393224 | tf_op jit(solution)/shard_map/ppermute | solution.py:220
  9.1 0.7 %collective-permute-start.4 = (bf16[128,512]{1,0:T(8,128)(2,1)S(1)}, bf16[128,512]{1,0:T(8,128)(2,1)S(1)}, u32[]{:S(2)}, u32[]{:S(2)}) collective-permute-start(bf16[128,512]{1,0:T(8,128)(2,1)S(1)} %get-tuple-element.14), channel_id=1, source_target_pairs={{12,4},{4,12},{13,5},{5,13},{14,6},{6,14},{15,7},{7,15},{28,20},{2... | collective-permute-start | bytes 393224 | tf_op jit(solution)/shard_map/ppermute | solution.py:220
  9.8 0.8 %collective-permute-done.1.near_ref = bf16[64,1024]{1,0:T(8,128)(2,1)S(1)} collective-permute-done((bf16[64,1024]{1,0:T(8,128)(2,1)S(1)}, bf16[64,1024]{1,0:T(8,128)(2,1)S(1)}, u32[]{:S(2)}, u32[]{:S(2)}) %collective-permute-start.1) | collective-permute-done | bytes 131104 | tf_op jit(solution)/shard_map/ppermute | solution.py:200
  10.7 0.1 collective-permute-start.2
  10.8 0.0 copy-done
  10.8 0.8 %shard_map.64.bias_ref = f32[128,384]{1,0:T(8,128)S(1)} custom-call(s32[12]{0:T(128)} %len_ref.1), custom_call_target="tpu_custom_call" | custom-call | tf_op jit(solution)/shard_map/pallas_call | solution.py:190
  11.6 0.4 %collective-permute-done.2.far_ref = bf16[64,512]{1,0:T(8,128)(2,1)S(1)} collective-permute-done((bf16[64,512]{1,0:T(8,128)(2,1)S(1)}, bf16[64,512]{1,0:T(8,128)(2,1)S(1)}, u32[]{:S(2)}, u32[]{:S(2)}) %collective-permute-start.2) | collective-permute-done | bytes 65568 | tf_op jit(solution)/shard_map/ppermute | solution.py:18
  12.0 2.7 %collective-permute-done.3.refs_0_ = bf16[128,512]{1,0:T(8,128)(2,1)S(1)} collective-permute-done((bf16[128,512]{1,0:T(8,128)(2,1)S(1)}, bf16[128,512]{1,0:T(8,128)(2,1)S(1)}, u32[]{:S(2)}, u32[]{:S(2)}) %collective-permute-start.3) | collective-permute-done | bytes 131104 | tf_op jit(solution)/shard_map/ppermute | solution.py:220
  14.7 0.0 collective-permute-done.4.refs_1_
  14.7 2.4 %shard_map.66 = bf16[128,2048]{1,0:T(8,128)(2,1)} custom-call(bf16[128,2048]{1,0:T(8,128)(2,1)S(1)} %constant_dynamic-slice_fusion.2.q_ref, f32[128,384]{1,0:T(8,128)S(1)} %shard_map.64.bias_ref, bf16[256,512]{1,0:T(8,128)(2,1)S(1)} %get-tuple-element.9.own_ref, bf16[256,512]{1,0:T(8,128)(2,1)S(1)} %collective-permute-done.peer_ref, ...), custom_call_target="tpu_custom_call" | custom-call | tf_op jit(solution)/shard_map/pallas_call | solution.py:237
  (5 shorter events, 0.1 us)
Async XLA Ops:
  0.0 10.8 %copy-start = (bf16[128,4096]{1,0:T(8,128)(2,1)S(1)}, bf16[128,4096]{1,0:T(8,128)(2,1)}, u32[]{:S(2)}) copy-start(bf16[128,4096]{1,0:T(8,128)(2,1)} %param.6) | copy-start | bytes 3145732
  1.4 3.2 %collective-permute-start = (bf16[256,512]{1,0:T(8,128)(2,1)S(1)}, bf16[256,512]{1,0:T(8,128)(2,1)S(1)}, u32[]{:S(2)}, u32[]{:S(2)}) collective-permute-start(bf16[256,512]{1,0:T(8,128)(2,1)S(1)} %get-tuple-element.10), channel_id=1, source_target_pairs={{0,1},{1,0},{2,3},{3,2},{4,5},{5,4},{6,7},{7,6},{8,9},{9,8},{10,11... | collective-permute-start | bytes 786440 | tf_op jit(solution)/shard_map/ppermute | solution.py:18
  1.9 8.8 %collective-permute-start.1 = (bf16[64,1024]{1,0:T(8,128)(2,1)S(1)}, bf16[64,1024]{1,0:T(8,128)(2,1)S(1)}, u32[]{:S(2)}, u32[]{:S(2)}) collective-permute-start(bf16[64,1024]{1,0:T(8,128)(2,1)S(1)} %get-tuple-element.11), channel_id=1, source_target_pairs={{0,4},{4,8},{8,12},{12,0},{1,5},{5,9},{9,13},{13,1},{2,6},{6,10},{... | collective-permute-start | bytes 393224 | tf_op jit(solution)/shard_map/ppermute | solution.py:200
  4.6 10.0 %collective-permute-start.3 = (bf16[128,512]{1,0:T(8,128)(2,1)S(1)}, bf16[128,512]{1,0:T(8,128)(2,1)S(1)}, u32[]{:S(2)}, u32[]{:S(2)}) collective-permute-start(bf16[128,512]{1,0:T(8,128)(2,1)S(1)} %get-tuple-element.13), channel_id=1, source_target_pairs={{12,0},{0,8},{13,1},{1,9},{14,2},{2,10},{15,3},{3,11},{28,16},{16,... | collective-permute-start | bytes 393224 | tf_op jit(solution)/shard_map/ppermute | solution.py:220
  9.1 5.5 %collective-permute-start.4 = (bf16[128,512]{1,0:T(8,128)(2,1)S(1)}, bf16[128,512]{1,0:T(8,128)(2,1)S(1)}, u32[]{:S(2)}, u32[]{:S(2)}) collective-permute-start(bf16[128,512]{1,0:T(8,128)(2,1)S(1)} %get-tuple-element.14), channel_id=1, source_target_pairs={{12,4},{4,12},{13,5},{5,13},{14,6},{6,14},{15,7},{7,15},{28,20},{2... | collective-permute-start | bytes 393224 | tf_op jit(solution)/shard_map/ppermute | solution.py:220
  10.7 1.3 %collective-permute-start.2 = (bf16[64,512]{1,0:T(8,128)(2,1)S(1)}, bf16[64,512]{1,0:T(8,128)(2,1)S(1)}, u32[]{:S(2)}, u32[]{:S(2)}) collective-permute-start(bf16[64,512]{1,0:T(8,128)(2,1)S(1)} %pad_maximum_fusion.1), channel_id=1, source_target_pairs={{0,1},{1,0},{2,3},{3,2},{4,5},{5,4},{6,7},{7,6},{8,9},{9,8},{10,11... | collective-permute-start | bytes 196616 | tf_op jit(solution)/shard_map/ppermute | solution.py:18

commit v4 on v3

--- a/solution.py
+++ b/solution.py
@@ -12,20 +12,22 @@
 NEG_FILL = -1e30
 SCORE_SCALE = HEAD_DIM ** (-0.5)
 EXP2_SCALE = SCORE_SCALE * math.log2(math.e)
+HEADS_AT_ONCE = 8
 
 
 def swap_cores(x):
     return lax.ppermute(x, "sub", [(0, 1), (1, 0)])
 
 
-def pack_kernel(n_ctx, k_ref, v_ref, ck_ref, cv_ref, raw_ref, mine_ref, theirs_ref, sems):
+def pack_kernel(n_ctx, first_sender, k_ref, v_ref, ck_ref, cv_ref, raw_ref, mine_ref, theirs_ref, sems):
     sub_pos = lax.axis_index("sub")
     last = lax.axis_index("ctx") == n_ctx - 1
     stretch_part, all_cols = k_ref.shape
     cache_part = ck_ref.shape[0]
     kv_cols = mine_ref.shape[1] // 2
     split = kv_cols != all_cols
-    copies = []
+    sends_cached = lax.axis_index("ctx") >= first_sender
+    copies, cached = [], []
     for i, (own_src, cache_src) in enumerate([(k_ref, ck_ref), (v_ref, cv_ref)]):
         dst = raw_ref.at[:, pl.ds(i * all_cols, all_cols)]
         from_own = pltpu.make_async_copy(own_src, dst, sems.at[0, i])
@@ -48,10 +50,16 @@
                 dst.at[pl.ds(row, rows), pl.ds(col, kv_cols)],
                 sems.at[out, i],
             )
-            copy.start()
-            copies.append(copy)
+            if i < 2:
+                copy.start()
+                copies.append(copy)
+            else:
+                pl.when(sends_cached)(copy.start)
+                cached.append(copy)
     for copy in copies:
         copy.wait()
+    for copy in cached:
+        pl.when(sends_cached)(copy.wait)
 
 
 def bias_kernel(prefix_len, stretch_part, cache_part, len_ref, bias_ref, lengths, sem):
@@ -87,18 +95,59 @@
         bias_ref[:, slot * tok_rows : (slot + 1) * tok_rows] = jnp.where(allowed, 0.0, NEG_FILL)
 
 
-def window_kernel(picks, q_ref, bias_ref, own_ref, peer_ref, near_ref, far_ref, *refs):
-    later_refs, o_ref = refs[:-1], refs[-1]
-    ctx_pos = lax.axis_index("ctx")
+def stacked(ref, heads):
+    return jnp.concatenate([ref[:, h * HEAD_DIM : (h + 1) * HEAD_DIM] for h in heads], axis=0)
+
+
+def attend(q_ref, bias, block, group, heads):
+    kv_cols = block.shape[1] // 2
+    at = group * HEAD_DIM
+    keys, values = block[:, at : at + HEAD_DIM], block[:, kv_cols + at : kv_cols + at + HEAD_DIM]
+    scores = lax.dot_general(
+        stacked(q_ref, heads), keys, (((1,), (1,)), ((), ())), preferred_element_type=jnp.float32
+    )
+    scores = scores.reshape(len(heads), *bias.shape) + bias[None]
+    ones = jnp.ones_like(values)
+    return scores.reshape(-1, bias.shape[1]), jnp.concatenate([values, ones], axis=1)
+
+
+def weigh(scores, row_max, values):
+    rounded = jnp.exp2((scores - row_max) * EXP2_SCALE).astype(jnp.bfloat16)
+    summed = jnp.dot(rounded, values, preferred_element_type=jnp.float32)
+    return summed[:, :HEAD_DIM], summed[:, HEAD_DIM:]
+
+
+def near_kernel(q_ref, bias_ref, own_ref, peer_ref, near_ref, far_ref, max_ref, sum_ref, out_ref):
     stretch_part, kv_cols = near_ref.shape[0], own_ref.shape[1] // 2
-    own = own_ref[:stretch_part], peer_ref[:stretch_part]
     all_cols = near_ref.shape[1] // 2
     at = [0, all_cols]
     if all_cols != kv_cols:
         at = [pl.multiple_of(lax.axis_index("sub") * kv_cols + x, HEAD_DIM) for x in at]
     near = jnp.concatenate([near_ref[:, pl.ds(x, kv_cols)] for x in at], axis=1)
-    blocks = [jnp.concatenate(own, axis=0), jnp.concatenate([near, far_ref[...]], axis=0)]
-    blocks += [None] * (bias_ref.shape[1] // q_ref.shape[0] - 2)
+    block = jnp.concatenate(
+        [own_ref[:stretch_part], peer_ref[:stretch_part], near, far_ref[...]], axis=0
+    )
+    tok_rows, head_cols = q_ref.shape
+    per_group = head_cols // kv_cols
+    bias = bias_ref[:, : block.shape[0]]
+    for first in range(0, head_cols // HEAD_DIM, HEADS_AT_ONCE):
+        heads = range(first, min(first + HEADS_AT_ONCE, head_cols // HEAD_DIM))
+        scores, values = attend(q_ref, bias, block, first // per_group, heads)
+        row_max = jnp.max(scores, axis=1, keepdims=True)
+        weighted, row_sum = weigh(scores, row_max, values)
+        row_max = jnp.broadcast_to(row_max, weighted.shape)
+        for i, head in enumerate(heads):
+            here, rows = pl.ds(head * HEAD_DIM, HEAD_DIM), slice(i * tok_rows, (i + 1) * tok_rows)
+            max_ref[:, here] = row_max[rows]
+            sum_ref[:, here] = row_sum[rows]
+            out_ref[:, here] = weighted[rows]
+
+
+def later_kernel(picks, q_ref, bias_ref, max_ref, sum_ref, weighted_ref, *refs):
+    later_refs, (o_ref, out, sems) = refs[:-3], refs[-3:]
+    ctx_pos = lax.axis_index("ctx")
+    tok_rows, head_cols = q_ref.shape
+    blocks = [None] * (bias_ref.shape[1] // tok_rows)
     for later_ref, pick in zip(later_refs, picks):
         for slot in sorted({slot for _, slot in pick}):
             here = [ctx_pos == dest for dest, at in pick if at == slot]
@@ -106,28 +155,30 @@
             if blocks[slot] is not None:
                 block = jnp.where(functools.reduce(jnp.logical_or, here), block, blocks[slot])
             blocks[slot] = block
-    group_count = kv_cols // HEAD_DIM
-    per_group = q_ref.shape[1] // kv_cols
-    ones = jnp.ones((bias_ref.shape[1], HEAD_DIM), jnp.bfloat16)
-    for group in range(group_count):
-        at = group * HEAD_DIM
-        keys = jnp.concatenate([b[:, at : at + HEAD_DIM] for b in blocks], axis=0)
-        at = at + kv_cols
-        values = jnp.concatenate([b[:, at : at + HEAD_DIM] for b in blocks], axis=0)
-        values = jnp.concatenate([values, ones], axis=1)
-        for head in range(group * per_group, (group + 1) * per_group):
+    block = jnp.concatenate(blocks[2:], axis=0)
+    per_group = head_cols // (block.shape[1] // 2)
+    bias = bias_ref[:, 2 * tok_rows :]
+    copies = []
+    for first in range(0, head_cols // HEAD_DIM, HEADS_AT_ONCE):
+        heads = range(first, min(first + HEADS_AT_ONCE, head_cols // HEAD_DIM))
+        scores, values = attend(q_ref, bias, block, first // per_group, heads)
+        old_max = stacked(max_ref, heads)
+        row_max = jnp.maximum(old_max, jnp.max(scores, axis=1, keepdims=True))
+        wide_max = jnp.concatenate([row_max] * (block.shape[0] // HEAD_DIM), axis=1)
+        weighted, row_sum = weigh(scores, wide_max, values)
+        shrink = jnp.exp2((old_max - row_max) * EXP2_SCALE)
+        weighted = stacked(weighted_ref, heads) * shrink + weighted
+        row_sum = stacked(sum_ref, heads) * shrink + row_sum
+        result = (weighted * pl.reciprocal(row_sum, approx=True)).astype(out.dtype)
+        for i, head in enumerate(heads):
             here = pl.ds(head * HEAD_DIM, HEAD_DIM)
-            scores = lax.dot_general(
-                q_ref[:, here],
-                keys,
-                (((1,), (1,)), ((), ())),
-                preferred_element_type=jnp.float32,
-            )
-            scores = scores + bias_ref[...]
-            row_max = jnp.max(scores, axis=1, keepdims=True)
-            rounded = jnp.exp2((scores - row_max) * EXP2_SCALE).astype(jnp.bfloat16)
-            summed = jnp.dot(rounded, values, preferred_element_type=jnp.float32)
-            o_ref[:, here] = (summed[:, :HEAD_DIM] / summed[:, HEAD_DIM:]).astype(o_ref.dtype)
+            out[:, here] = result[i * tok_rows : (i + 1) * tok_rows]
+        here = pl.ds(first * HEAD_DIM, len(heads) * HEAD_DIM)
+        copy = pltpu.make_async_copy(out.at[:, here], o_ref.at[:, here], sems.at[len(copies)])
+        copy.start()
+        copies.append(copy)
+    for copy in copies:
+        copy.wait()
 
 
 def plan_rounds(n_ctx, reach, tok_rows, cache_part, shard_rows):
@@ -176,9 +227,11 @@
     def in_hbm(*arrays):
         return [pltpu.with_memory_space_constraint(x, pltpu.HBM) for x in arrays]
 
+    rounds = plan_rounds(n_ctx, reach, tok_rows, cache_part, cache_part * n_sub)
+    first_sender = min(src for step in rounds for src, sent in step.items() if sent[0] is not None)
     half = jax.ShapeDtypeStruct((stretch_part + cache_part, 2 * kv_cols), stretch_keys.dtype)
     raw, mine, theirs = pl.pallas_call(
-        functools.partial(pack_kernel, n_ctx),
+        functools.partial(pack_kernel, n_ctx, first_sender),
         out_shape=[
             jax.ShapeDtypeStruct((stretch_part, 2 * all_cols), stretch_keys.dtype), half, half
         ],
@@ -210,7 +263,7 @@
 
     own = jnp.concatenate([mine[:stretch_part], peers[:stretch_part]])
     sent, later, picks = [], [], []
-    for step in plan_rounds(n_ctx, reach, tok_rows, cache_part, cache_part * n_sub):
+    for step in rounds:
         block = own
         for source, (row, _, _) in step.items():
             if row is not None:
@@ -234,13 +287,27 @@
         near_theirs = near
     far = swap_cores(near_theirs)
     mine_q = lax.dynamic_slice_in_dim(queries, sub_pos * head_cols, head_cols, 1)
+    head_count = head_cols // HEAD_DIM
+    state = jax.ShapeDtypeStruct((tok_rows, head_cols), jnp.float32)
+    large = pltpu.CompilerParams(vmem_limit_bytes=24 << 20)
+    row_max, row_sum, weighted = pl.pallas_call(
+        near_kernel,
+        out_shape=[state] * 3,
+        in_specs=[vmem] * 6,
+        out_specs=[vmem] * 3,
+        compiler_params=large,
+    )(mine_q, bias, mine, peers, near, far)
     return pl.pallas_call(
-        functools.partial(window_kernel, picks),
+        functools.partial(later_kernel, picks),
         out_shape=jax.ShapeDtypeStruct((tok_rows, head_cols), queries.dtype),
-        in_specs=[vmem] * (6 + len(later)),
-        out_specs=vmem,
-        compiler_params=pltpu.CompilerParams(vmem_limit_bytes=24 << 20),
-    )(mine_q, bias, mine, peers, near, far, *later)
+        in_specs=[vmem] * (5 + len(later)),
+        out_specs=hbm,
+        scratch_shapes=[
+            pltpu.VMEM((tok_rows, head_cols), queries.dtype),
+            pltpu.SemaphoreType.DMA((pl.cdiv(head_count, HEADS_AT_ONCE),)),
+        ],
+        compiler_params=large,
+    )(mine_q, bias, row_max, row_sum, weighted, *later)
 
 
 def solution(mesh):

time: 17.2 us -> 16.3 us (0.948)
  the two profiles are of different devices: /device:TPU:0 before, /device:TPU:25 now
where the time goes in v4:
time: 16.3 us; the launch traced here: 16.1 us
  waiting for transfers between devices  5.88 us (36%)
  starting transfers between devices  5.32 us (33%)
  Pallas kernels  4.73 us (29%)
    ppermute x2, waiting for transfers between devices, on_device(): later.append(lax.ppermute(block, 'ctx', pairs))  4.49 us
    ppermute x2, starting transfers between devices, on_device(): later.append(lax.ppermute(block, 'ctx', pairs))  3.66 us
    pallas_call x1, Pallas kernels, on_device(): pl.pallas_call(functools.partial(later_kernel, picks), out_shape=jax.Shap...  1.71 us
    ppermute x2, starting transfers between devices, swap_cores(): return lax.ppermute(x, 'sub', [(0, 1), (1, 0)])  1.66 us
    pallas_call x1, Pallas kernels, on_device(): pl.pallas_call(functools.partial(pack_kernel, n_ctx, first_sender), out_s...  1.35 us
    ppermute x2, waiting for transfers between devices, swap_cores(): return lax.ppermute(x, 'sub', [(0, 1), (1, 0)])  1.25 us
    pallas_call x1, Pallas kernels, on_device(): pl.pallas_call(near_kernel, out_shape=[state] * 3, in_specs=[vmem] * 6, o...  0.91 us
    pallas_call x1, Pallas kernels, on_device(): pl.pallas_call(functools.partial(bias_kernel, prefix_len, stretch_part, c...  0.75 us
  transfers between devices with their start and end apart: 5, of which 4 were waited for; matrix products, arithmetic and copies ran while one was open for 1% of the time, Pallas kernels for 10%

profile of v4, /device:TPU:25, one launch (start us, length us, event | category | flops | bytes accessed | tf_op | source)
XLA Modules:
  0.0 16.1 jit_solution(5313336810300360392)
XLA Ops:
  0.0 0.0 copy-start
  0.0 1.4 %shard_map.65 = (bf16[64,1024]{1,0:T(8,128)(2,1)S(1)}, bf16[256,512]{1,0:T(8,128)(2,1)S(1)}, bf16[256,512]{1,0:T(8,128)(2,1)S(1)}) custom-call(bf16[64,512]{1,0:T(8,128)(2,1)} %k_ref.1, bf16[64,512]{1,0:T(8,128)(2,1)} %v_ref.1, bf16[192,512]{1,0:T(8,128)(2,1)} %ck_ref.1, bf16[192,512]{1,0:T(8,128)(2,1)} %cv_ref.1), custom_call_target="tpu_custom_call" | custom-call | tf_op jit(solution)/shard_map/pallas_call | solution.py:233
  1.4 0.7 %collective-permute-start = (bf16[256,512]{1,0:T(8,128)(2,1)S(1)}, bf16[256,512]{1,0:T(8,128)(2,1)S(1)}, u32[]{:S(2)}, u32[]{:S(2)}) collective-permute-start(bf16[256,512]{1,0:T(8,128)(2,1)S(1)} %get-tuple-element.13), channel_id=1, source_target_pairs={{0,1},{1,0},{2,3},{3,2},{4,5},{5,4},{6,7},{7,6},{8,9},{9,8},{10,11... | collective-permute-start | bytes 786440 | tf_op jit(solution)/shard_map/ppermute | solution.py:19
  2.1 0.0 collective-permute-start.1
  2.1 1.1 %collective-permute-done.peer_ref = bf16[256,512]{1,0:T(8,128)(2,1)S(1)} collective-permute-done((bf16[256,512]{1,0:T(8,128)(2,1)S(1)}, bf16[256,512]{1,0:T(8,128)(2,1)S(1)}, u32[]{:S(2)}, u32[]{:S(2)}) %collective-permute-start) | collective-permute-done | bytes 262176 | tf_op jit(solution)/shard_map/ppermute | solution.py:19
  3.3 0.1 fusion
  3.4 1.7 %collective-permute-start.3 = (bf16[128,512]{1,0:T(8,128)(2,1)S(1)}, bf16[128,512]{1,0:T(8,128)(2,1)S(1)}, u32[]{:S(2)}, u32[]{:S(2)}) collective-permute-start(bf16[128,512]{1,0:T(8,128)(2,1)S(1)} %get-tuple-element.19), channel_id=1, source_target_pairs={{12,0},{0,8},{13,1},{1,9},{14,2},{2,10},{15,3},{3,11},{28,16},{16,... | collective-permute-start | bytes 393224 | tf_op jit(solution)/shard_map/ppermute | solution.py:273
  5.1 1.9 %collective-permute-start.4 = (bf16[128,512]{1,0:T(8,128)(2,1)S(1)}, bf16[128,512]{1,0:T(8,128)(2,1)S(1)}, u32[]{:S(2)}, u32[]{:S(2)}) collective-permute-start(bf16[128,512]{1,0:T(8,128)(2,1)S(1)} %get-tuple-element.20), channel_id=1, source_target_pairs={{12,4},{4,12},{13,5},{5,13},{14,6},{6,14},{15,7},{7,15},{28,20},{2... | collective-permute-start | bytes 393224 | tf_op jit(solution)/shard_map/ppermute | solution.py:273
  7.0 0.1 collective-permute-done.1.near_ref
  7.2 0.9 %collective-permute-start.2 = (bf16[64,512]{1,0:T(8,128)(2,1)S(1)}, bf16[64,512]{1,0:T(8,128)(2,1)S(1)}, u32[]{:S(2)}, u32[]{:S(2)}) collective-permute-start(bf16[64,512]{1,0:T(8,128)(2,1)S(1)} %pad_maximum_fusion.1), channel_id=1, source_target_pairs={{0,1},{1,0},{2,3},{3,2},{4,5},{5,4},{6,7},{7,6},{8,9},{9,8},{10,11... | collective-permute-start | bytes 196616 | tf_op jit(solution)/shard_map/ppermute | solution.py:19
  8.1 0.0 copy-done
  8.2 0.8 %shard_map.64.bias_ref = f32[128,384]{1,0:T(8,128)S(1)} custom-call(s32[12]{0:T(128)} %len_ref.1), custom_call_target="tpu_custom_call" | custom-call | tf_op jit(solution)/shard_map/pallas_call | solution.py:243
  8.9 0.1 collective-permute-done.2.far_ref
  9.0 0.9 %shard_map.66 = (f32[128,2048]{1,0:T(8,128)S(1)}, f32[128,2048]{1,0:T(8,128)S(1)}, f32[128,2048]{1,0:T(8,128)S(1)}) custom-call(bf16[128,2048]{1,0:T(8,128)(2,1)S(1)} %constant_dynamic-slice_fusion.2.q_ref, f32[128,384]{1,0:T(8,128)S(1)} %shard_map.64.bias_ref, bf16[256,512]{1,0:T(8,128)(2,1)S(1)} %get-tuple-element.12.own_ref, ...), custom_call_target="tpu_custom_call" | custom-call | tf_op jit(solution)/shard_map/pallas_call | solution.py:293
  9.9 0.0 collective-permute-done.3.refs_0_
  9.9 4.5 %collective-permute-done.4.refs_1_ = bf16[128,512]{1,0:T(8,128)(2,1)S(1)} collective-permute-done((bf16[128,512]{1,0:T(8,128)(2,1)S(1)}, bf16[128,512]{1,0:T(8,128)(2,1)S(1)}, u32[]{:S(2)}, u32[]{:S(2)}) %collective-permute-start.4) | collective-permute-done | bytes 131104 | tf_op jit(solution)/shard_map/ppermute | solution.py:273
  14.4 1.7 %shard_map.67 = bf16[128,2048]{1,0:T(8,128)(2,1)} custom-call(bf16[128,2048]{1,0:T(8,128)(2,1)S(1)} %constant_dynamic-slice_fusion.2.q_ref, f32[128,384]{1,0:T(8,128)S(1)} %shard_map.64.bias_ref, f32[128,2048]{1,0:T(8,128)S(1)} %get-tuple-element.16.max_ref, f32[128,2048]{1,0:T(8,128)S(1)} %get-tuple-element.17.sum_ref, ...), custom_call_target="tpu_custom_call" | custom-call | tf_op jit(solution)/shard_map/pallas_call | solution.py:300
  (5 shorter events, 0.1 us)
Async XLA Ops:
  0.0 8.1 %copy-start = (bf16[128,4096]{1,0:T(8,128)(2,1)S(1)}, bf16[128,4096]{1,0:T(8,128)(2,1)}, u32[]{:S(2)}) copy-start(bf16[128,4096]{1,0:T(8,128)(2,1)} %param.6) | copy-start | bytes 3145732
  1.4 1.9 %collective-permute-start = (bf16[256,512]{1,0:T(8,128)(2,1)S(1)}, bf16[256,512]{1,0:T(8,128)(2,1)S(1)}, u32[]{:S(2)}, u32[]{:S(2)}) collective-permute-start(bf16[256,512]{1,0:T(8,128)(2,1)S(1)} %get-tuple-element.13), channel_id=1, source_target_pairs={{0,1},{1,0},{2,3},{3,2},{4,5},{5,4},{6,7},{7,6},{8,9},{9,8},{10,11... | collective-permute-start | bytes 786440 | tf_op jit(solution)/shard_map/ppermute | solution.py:19
  2.1 5.1 %collective-permute-start.1 = (bf16[64,1024]{1,0:T(8,128)(2,1)S(1)}, bf16[64,1024]{1,0:T(8,128)(2,1)S(1)}, u32[]{:S(2)}, u32[]{:S(2)}) collective-permute-start(bf16[64,1024]{1,0:T(8,128)(2,1)S(1)} %get-tuple-element.14), channel_id=1, source_target_pairs={{0,4},{4,8},{8,12},{12,0},{1,5},{5,9},{9,13},{13,1},{2,6},{6,10},{... | collective-permute-start | bytes 393224 | tf_op jit(solution)/shard_map/ppermute | solution.py:253
  3.4 6.6 %collective-permute-start.3 = (bf16[128,512]{1,0:T(8,128)(2,1)S(1)}, bf16[128,512]{1,0:T(8,128)(2,1)S(1)}, u32[]{:S(2)}, u32[]{:S(2)}) collective-permute-start(bf16[128,512]{1,0:T(8,128)(2,1)S(1)} %get-tuple-element.19), channel_id=1, source_target_pairs={{12,0},{0,8},{13,1},{1,9},{14,2},{2,10},{15,3},{3,11},{28,16},{16,... | collective-permute-start | bytes 393224 | tf_op jit(solution)/shard_map/ppermute | solution.py:273
  5.1 9.3 %collective-permute-start.4 = (bf16[128,512]{1,0:T(8,128)(2,1)S(1)}, bf16[128,512]{1,0:T(8,128)(2,1)S(1)}, u32[]{:S(2)}, u32[]{:S(2)}) collective-permute-start(bf16[128,512]{1,0:T(8,128)(2,1)S(1)} %get-tuple-element.20), channel_id=1, source_target_pairs={{12,4},{4,12},{13,5},{5,13},{14,6},{6,14},{15,7},{7,15},{28,20},{2... | collective-permute-start | bytes 393224 | tf_op jit(solution)/shard_map/ppermute | solution.py:273
  7.2 1.8 %collective-permute-start.2 = (bf16[64,512]{1,0:T(8,128)(2,1)S(1)}, bf16[64,512]{1,0:T(8,128)(2,1)S(1)}, u32[]{:S(2)}, u32[]{:S(2)}) collective-permute-start(bf16[64,512]{1,0:T(8,128)(2,1)S(1)} %pad_maximum_fusion.1), channel_id=1, source_target_pairs={{0,1},{1,0},{2,3},{3,2},{4,5},{5,4},{6,7},{7,6},{8,9},{9,8},{10,11... | collective-permute-start | bytes 196616 | tf_op jit(solution)/shard_map/ppermute | solution.py:19

commit v5 on v4

--- a/solution.py
+++ b/solution.py
@@ -13,6 +13,7 @@
 SCORE_SCALE = HEAD_DIM ** (-0.5)
 EXP2_SCALE = SCORE_SCALE * math.log2(math.e)
 HEADS_AT_ONCE = 8
+LATER_HEADS = 2
 
 
 def swap_cores(x):
@@ -145,12 +146,12 @@
 
 def later_kernel(picks, q_ref, bias_ref, max_ref, sum_ref, weighted_ref, *refs):
     later_refs, (o_ref, out, sems) = refs[:-3], refs[-3:]
-    ctx_pos = lax.axis_index("ctx")
+    ctx_pos, sub_pos = lax.axis_index("ctx"), lax.axis_index("sub")
     tok_rows, head_cols = q_ref.shape
     blocks = [None] * (bias_ref.shape[1] // tok_rows)
     for later_ref, pick in zip(later_refs, picks):
-        for slot in sorted({slot for _, slot in pick}):
-            here = [ctx_pos == dest for dest, at in pick if at == slot]
+        for slot in sorted({slot for _, _, slot in pick}):
+            here = [(ctx_pos == dest) & (sub_pos == sub) for dest, sub, at in pick if at == slot]
             block = later_ref[...]
             if blocks[slot] is not None:
                 block = jnp.where(functools.reduce(jnp.logical_or, here), block, blocks[slot])
@@ -158,10 +159,14 @@
     block = jnp.concatenate(blocks[2:], axis=0)
     per_group = head_cols // (block.shape[1] // 2)
     bias = bias_ref[:, 2 * tok_rows :]
+    head_count = head_cols // HEAD_DIM
+    batches = [
+        range(first, min(first + LATER_HEADS, head_count))
+        for first in range(0, head_count, LATER_HEADS)
+    ]
+    attended = [attend(q_ref, bias, block, heads[0] // per_group, heads) for heads in batches]
     copies = []
-    for first in range(0, head_cols // HEAD_DIM, HEADS_AT_ONCE):
-        heads = range(first, min(first + HEADS_AT_ONCE, head_cols // HEAD_DIM))
-        scores, values = attend(q_ref, bias, block, first // per_group, heads)
+    for heads, (scores, values) in zip(batches, attended):
         old_max = stacked(max_ref, heads)
         row_max = jnp.maximum(old_max, jnp.max(scores, axis=1, keepdims=True))
         wide_max = jnp.concatenate([row_max] * (block.shape[0] // HEAD_DIM), axis=1)
@@ -173,7 +178,7 @@
         for i, head in enumerate(heads):
             here = pl.ds(head * HEAD_DIM, HEAD_DIM)
             out[:, here] = result[i * tok_rows : (i + 1) * tok_rows]
-        here = pl.ds(first * HEAD_DIM, len(heads) * HEAD_DIM)
+        here = pl.ds(heads[0] * HEAD_DIM, len(heads) * HEAD_DIM)
         copy = pltpu.make_async_copy(out.at[:, here], o_ref.at[:, here], sems.at[len(copies)])
         copy.start()
         copies.append(copy)
@@ -181,7 +186,7 @@
         copy.wait()
 
 
-def plan_rounds(n_ctx, reach, tok_rows, cache_part, shard_rows):
+def plan_rounds(n_ctx, n_sub, reach, tok_rows, cache_part, shard_rows):
     per_shard = shard_rows // tok_rows
     cached, stretch = [], []
     for dest in range(n_ctx):
@@ -197,13 +202,17 @@
             cached.append((source, row, dest, slot))
     rounds = []
     for source, row, dest, slot in cached + stretch:
-        dests = [{d for _, d, _ in step.values()} for step in rounds]
-        free = [i for i, step in enumerate(rounds) if source not in step and dest not in dests[i]]
-        free.sort(key=lambda i: source not in dests[i])
-        if not free:
-            rounds.append({})
-            free = [len(rounds) - 1]
-        rounds[free[0]][source] = (row, dest, slot)
+        for sub in range(n_sub):
+            dests = [{(d, i) for (_, i), (_, d, _) in step.items()} for step in rounds]
+            free = [
+                i for i, step in enumerate(rounds)
+                if (source, sub) not in step and (dest, sub) not in dests[i]
+            ]
+            free.sort(key=lambda i: ((source, sub) in dests[i]) == (sub > 0))
+            if not free:
+                rounds.append({})
+                free = [len(rounds) - 1]
+            rounds[free[0]][source, sub] = (row, dest, slot)
     return rounds
 
 
@@ -227,8 +236,8 @@
     def in_hbm(*arrays):
         return [pltpu.with_memory_space_constraint(x, pltpu.HBM) for x in arrays]
 
-    rounds = plan_rounds(n_ctx, reach, tok_rows, cache_part, cache_part * n_sub)
-    first_sender = min(src for step in rounds for src, sent in step.items() if sent[0] is not None)
+    rounds = plan_rounds(n_ctx, n_sub, reach, tok_rows, cache_part, cache_part * n_sub)
+    first_sender = min(src for step in rounds for (src, _), leg in step.items() if leg[0] is not None)
     half = jax.ShapeDtypeStruct((stretch_part + cache_part, 2 * kv_cols), stretch_keys.dtype)
     raw, mine, theirs = pl.pallas_call(
         functools.partial(pack_kernel, n_ctx, first_sender),
@@ -265,13 +274,12 @@
     sent, later, picks = [], [], []
     for step in rounds:
         block = own
-        for source, (row, _, _) in step.items():
-            if row is not None:
-                block = jnp.where(ctx_pos == source, cached_rows(row), block)
-        pairs = [(source, dest) for source, (_, dest, _) in step.items()]
+        for source, row in sorted({(src, leg[0]) for (src, _), leg in step.items() if leg[0] is not None}):
+            block = jnp.where(ctx_pos == source, cached_rows(row), block)
+        pairs = [(src * n_sub + sub, leg[1] * n_sub + sub) for (src, sub), leg in step.items()]
         sent.append(block)
-        later.append(lax.ppermute(block, "ctx", pairs))
-        picks.append([(dest, slot) for _, dest, slot in step.values()])
+        later.append(lax.ppermute(block, ("ctx", "sub"), pairs))
+        picks.append([(dest, sub, slot) for (_, sub), (_, dest, slot) in step.items()])
 
     near, *_ = lax.optimization_barrier((near, *sent[::-1]))
     if kv_cols != all_cols:
@@ -304,7 +312,7 @@
         out_specs=hbm,
         scratch_shapes=[
             pltpu.VMEM((tok_rows, head_cols), queries.dtype),
-            pltpu.SemaphoreType.DMA((pl.cdiv(head_count, HEADS_AT_ONCE),)),
+            pltpu.SemaphoreType.DMA((pl.cdiv(head_count, LATER_HEADS),)),
         ],
         compiler_params=large,
     )(mine_q, bias, row_max, row_sum, weighted, *later)

time: 16.3 us -> 16 us (0.982)
  the two profiles are of different devices: /device:TPU:25 before, /device:TPU:15 now
where the time goes in v5:
time: 16 us; the launch traced here: 15.8 us
  starting transfers between devices  9.08 us (57%)
  Pallas kernels  4.32 us (27%)
  waiting for transfers between devices  2.14 us (13%)
    ppermute x2, starting transfers between devices, on_device(): later.append(lax.ppermute(block, ('ctx', 'sub'), pairs))  5.63 us
    ppermute x2, starting transfers between devices, swap_cores(): return lax.ppermute(x, 'sub', [(0, 1), (1, 0)])  2.15 us
    ppermute x2, waiting for transfers between devices, on_device(): later.append(lax.ppermute(block, ('ctx', 'sub'), pairs))  2.03 us
    pallas_call x1, Pallas kernels, on_device(): pl.pallas_call(functools.partial(later_kernel, picks), out_shape=jax.Shap...  1.59 us
    ppermute x1, starting transfers between devices, on_device(): lax.ppermute(raw, 'ctx', [(i, (i + 1) % n_ctx) for i in range(n_ctx)])  1.3 us
    pallas_call x1, Pallas kernels, on_device(): pl.pallas_call(functools.partial(pack_kernel, n_ctx, first_sender), out_s...  1.07 us
    pallas_call x1, Pallas kernels, on_device(): pl.pallas_call(near_kernel, out_shape=[state] * 3, in_specs=[vmem] * 6, o...  0.91 us
    pallas_call x1, Pallas kernels, on_device(): pl.pallas_call(functools.partial(bias_kernel, prefix_len, stretch_part, c...  0.75 us
  transfers between devices with their start and end apart: 5, of which 3 were waited for; matrix products, arithmetic and copies ran while one was open for 1% of the time, Pallas kernels for 11%

profile of v5, /device:TPU:15, one launch (start us, length us, event | category | flops | bytes accessed | tf_op | source)
XLA Modules:
  0.0 15.8 jit_solution(17420438141306158086)
XLA Ops:
  0.0 0.0 copy-start
  0.0 1.1 %shard_map.65 = (bf16[64,1024]{1,0:T(8,128)(2,1)S(1)}, bf16[256,512]{1,0:T(8,128)(2,1)S(1)}, bf16[256,512]{1,0:T(8,128)(2,1)S(1)}) custom-call(bf16[64,512]{1,0:T(8,128)(2,1)} %k_ref.1, bf16[64,512]{1,0:T(8,128)(2,1)} %v_ref.1, bf16[192,512]{1,0:T(8,128)(2,1)} %ck_ref.1, bf16[192,512]{1,0:T(8,128)(2,1)} %cv_ref.1), custom_call_target="tpu_custom_call" | custom-call | tf_op jit(solution)/shard_map/pallas_call | solution.py:242
  1.1 0.7 %collective-permute-start = (bf16[256,512]{1,0:T(8,128)(2,1)S(1)}, bf16[256,512]{1,0:T(8,128)(2,1)S(1)}, u32[]{:S(2)}, u32[]{:S(2)}) collective-permute-start(bf16[256,512]{1,0:T(8,128)(2,1)S(1)} %get-tuple-element.13), channel_id=1, source_target_pairs={{0,1},{1,0},{2,3},{3,2},{4,5},{5,4},{6,7},{7,6},{8,9},{9,8},{10,11... | collective-permute-start | bytes 786440 | tf_op jit(solution)/shard_map/ppermute | solution.py:20
  1.8 1.3 %collective-permute-start.1 = (bf16[64,1024]{1,0:T(8,128)(2,1)S(1)}, bf16[64,1024]{1,0:T(8,128)(2,1)S(1)}, u32[]{:S(2)}, u32[]{:S(2)}) collective-permute-start(bf16[64,1024]{1,0:T(8,128)(2,1)S(1)} %get-tuple-element.14), channel_id=1, source_target_pairs={{0,4},{4,8},{8,12},{12,0},{1,5},{5,9},{9,13},{13,1},{2,6},{6,10},{... | collective-permute-start | bytes 393224 | tf_op jit(solution)/shard_map/ppermute | solution.py:262
  3.1 0.0 collective-permute-done.peer_ref
  3.1 0.1 fusion
  3.2 4.3 %collective-permute-start.3 = (bf16[128,512]{1,0:T(8,128)(2,1)S(1)}, bf16[128,512]{1,0:T(8,128)(2,1)S(1)}, u32[]{:S(2)}, u32[]{:S(2)}) collective-permute-start(bf16[128,512]{1,0:T(8,128)(2,1)S(1)} %get-tuple-element.19), channel_id=1, source_target_pairs={{12,0},{13,1},{0,8},{5,13},{14,2},{15,3},{2,10},{7,15},{28,16},{29... | collective-permute-start | bytes 393224 | tf_op jit(solution)/shard_map/ppermute | solution.py:281
  7.6 1.3 %collective-permute-start.4 = (bf16[128,512]{1,0:T(8,128)(2,1)S(1)}, bf16[128,512]{1,0:T(8,128)(2,1)S(1)}, u32[]{:S(2)}, u32[]{:S(2)}) collective-permute-start(bf16[128,512]{1,0:T(8,128)(2,1)S(1)} %get-tuple-element.20), channel_id=1, source_target_pairs={{12,4},{13,5},{1,9},{4,12},{14,6},{15,7},{3,11},{6,14},{28,20},{29... | collective-permute-start | bytes 393224 | tf_op jit(solution)/shard_map/ppermute | solution.py:281
  8.9 0.0 collective-permute-done.1.near_ref
  8.9 1.4 %collective-permute-start.2 = (bf16[64,512]{1,0:T(8,128)(2,1)S(1)}, bf16[64,512]{1,0:T(8,128)(2,1)S(1)}, u32[]{:S(2)}, u32[]{:S(2)}) collective-permute-start(bf16[64,512]{1,0:T(8,128)(2,1)S(1)} %pad_maximum_fusion.1), channel_id=1, source_target_pairs={{0,1},{1,0},{2,3},{3,2},{4,5},{5,4},{6,7},{7,6},{8,9},{9,8},{10,11... | collective-permute-start | bytes 196616 | tf_op jit(solution)/shard_map/ppermute | solution.py:20
  10.3 0.0 copy-done
  10.4 0.8 %shard_map.64.bias_ref = f32[128,384]{1,0:T(8,128)S(1)} custom-call(s32[12]{0:T(128)} %len_ref.1), custom_call_target="tpu_custom_call" | custom-call | tf_op jit(solution)/shard_map/pallas_call | solution.py:252
  11.1 0.1 collective-permute-done.2.far_ref
  11.2 0.9 %shard_map.66 = (f32[128,2048]{1,0:T(8,128)S(1)}, f32[128,2048]{1,0:T(8,128)S(1)}, f32[128,2048]{1,0:T(8,128)S(1)}) custom-call(bf16[128,2048]{1,0:T(8,128)(2,1)S(1)} %constant_dynamic-slice_fusion.2.q_ref, f32[128,384]{1,0:T(8,128)S(1)} %shard_map.64.bias_ref, bf16[256,512]{1,0:T(8,128)(2,1)S(1)} %get-tuple-element.12.own_ref, ...), custom_call_target="tpu_custom_call" | custom-call | tf_op jit(solution)/shard_map/pallas_call | solution.py:301
  12.2 0.6 %collective-permute-done.3.refs_0_ = bf16[128,512]{1,0:T(8,128)(2,1)S(1)} collective-permute-done((bf16[128,512]{1,0:T(8,128)(2,1)S(1)}, bf16[128,512]{1,0:T(8,128)(2,1)S(1)}, u32[]{:S(2)}, u32[]{:S(2)}) %collective-permute-start.3) | collective-permute-done | bytes 131104 | tf_op jit(solution)/shard_map/ppermute | solution.py:281
  12.8 1.4 %collective-permute-done.4.refs_1_ = bf16[128,512]{1,0:T(8,128)(2,1)S(1)} collective-permute-done((bf16[128,512]{1,0:T(8,128)(2,1)S(1)}, bf16[128,512]{1,0:T(8,128)(2,1)S(1)}, u32[]{:S(2)}, u32[]{:S(2)}) %collective-permute-start.4) | collective-permute-done | bytes 131104 | tf_op jit(solution)/shard_map/ppermute | solution.py:281
  14.2 1.6 %shard_map.67 = bf16[128,2048]{1,0:T(8,128)(2,1)} custom-call(bf16[128,2048]{1,0:T(8,128)(2,1)S(1)} %constant_dynamic-slice_fusion.2.q_ref, f32[128,384]{1,0:T(8,128)S(1)} %shard_map.64.bias_ref, f32[128,2048]{1,0:T(8,128)S(1)} %get-tuple-element.16.max_ref, f32[128,2048]{1,0:T(8,128)S(1)} %get-tuple-element.17.sum_ref, ...), custom_call_target="tpu_custom_call" | custom-call | tf_op jit(solution)/shard_map/pallas_call | solution.py:308
  (5 shorter events, 0.1 us)
Async XLA Ops:
  0.0 10.3 %copy-start = (bf16[128,4096]{1,0:T(8,128)(2,1)S(1)}, bf16[128,4096]{1,0:T(8,128)(2,1)}, u32[]{:S(2)}) copy-start(bf16[128,4096]{1,0:T(8,128)(2,1)} %param.6) | copy-start | bytes 3145732
  1.1 2.0 %collective-permute-start = (bf16[256,512]{1,0:T(8,128)(2,1)S(1)}, bf16[256,512]{1,0:T(8,128)(2,1)S(1)}, u32[]{:S(2)}, u32[]{:S(2)}) collective-permute-start(bf16[256,512]{1,0:T(8,128)(2,1)S(1)} %get-tuple-element.13), channel_id=1, source_target_pairs={{0,1},{1,0},{2,3},{3,2},{4,5},{5,4},{6,7},{7,6},{8,9},{9,8},{10,11... | collective-permute-start | bytes 786440 | tf_op jit(solution)/shard_map/ppermute | solution.py:20
  1.8 7.1 %collective-permute-start.1 = (bf16[64,1024]{1,0:T(8,128)(2,1)S(1)}, bf16[64,1024]{1,0:T(8,128)(2,1)S(1)}, u32[]{:S(2)}, u32[]{:S(2)}) collective-permute-start(bf16[64,1024]{1,0:T(8,128)(2,1)S(1)} %get-tuple-element.14), channel_id=1, source_target_pairs={{0,4},{4,8},{8,12},{12,0},{1,5},{5,9},{9,13},{13,1},{2,6},{6,10},{... | collective-permute-start | bytes 393224 | tf_op jit(solution)/shard_map/ppermute | solution.py:262
  3.2 9.6 %collective-permute-start.3 = (bf16[128,512]{1,0:T(8,128)(2,1)S(1)}, bf16[128,512]{1,0:T(8,128)(2,1)S(1)}, u32[]{:S(2)}, u32[]{:S(2)}) collective-permute-start(bf16[128,512]{1,0:T(8,128)(2,1)S(1)} %get-tuple-element.19), channel_id=1, source_target_pairs={{12,0},{13,1},{0,8},{5,13},{14,2},{15,3},{2,10},{7,15},{28,16},{29... | collective-permute-start | bytes 393224 | tf_op jit(solution)/shard_map/ppermute | solution.py:281
  7.6 6.6 %collective-permute-start.4 = (bf16[128,512]{1,0:T(8,128)(2,1)S(1)}, bf16[128,512]{1,0:T(8,128)(2,1)S(1)}, u32[]{:S(2)}, u32[]{:S(2)}) collective-permute-start(bf16[128,512]{1,0:T(8,128)(2,1)S(1)} %get-tuple-element.20), channel_id=1, source_target_pairs={{12,4},{13,5},{1,9},{4,12},{14,6},{15,7},{3,11},{6,14},{28,20},{29... | collective-permute-start | bytes 393224 | tf_op jit(solution)/shard_map/ppermute | solution.py:281
  8.9 2.3 %collective-permute-start.2 = (bf16[64,512]{1,0:T(8,128)(2,1)S(1)}, bf16[64,512]{1,0:T(8,128)(2,1)S(1)}, u32[]{:S(2)}, u32[]{:S(2)}) collective-permute-start(bf16[64,512]{1,0:T(8,128)(2,1)S(1)} %pad_maximum_fusion.1), channel_id=1, source_target_pairs={{0,1},{1,0},{2,3},{3,2},{4,5},{5,4},{6,7},{7,6},{8,9},{9,8},{10,11... | collective-permute-start | bytes 196616 | tf_op jit(solution)/shard_map/ppermute | solution.py:20

commit v6 on v5

--- a/solution.py
+++ b/solution.py
@@ -20,47 +20,45 @@
     return lax.ppermute(x, "sub", [(0, 1), (1, 0)])
 
 
-def pack_kernel(n_ctx, first_sender, k_ref, v_ref, ck_ref, cv_ref, raw_ref, mine_ref, theirs_ref, sems):
-    sub_pos = lax.axis_index("sub")
-    last = lax.axis_index("ctx") == n_ctx - 1
+def pack_kernel(n_ctx, owners, k_ref, v_ref, ck_ref, cv_ref, raw_ref, mine_ref, theirs_ref, sems):
+    ctx_pos, sub_pos = lax.axis_index("ctx"), lax.axis_index("sub")
+    last = ctx_pos == n_ctx - 1
+    owns = functools.reduce(jnp.logical_or, [(ctx_pos == c) & (sub_pos == s) for c, s in owners])
     stretch_part, all_cols = k_ref.shape
     cache_part = ck_ref.shape[0]
     kv_cols = mine_ref.shape[1] // 2
-    split = kv_cols != all_cols
-    sends_cached = lax.axis_index("ctx") >= first_sender
-    copies, cached = [], []
     for i, (own_src, cache_src) in enumerate([(k_ref, ck_ref), (v_ref, cv_ref)]):
         dst = raw_ref.at[:, pl.ds(i * all_cols, all_cols)]
-        from_own = pltpu.make_async_copy(own_src, dst, sems.at[0, i])
+        from_own = pltpu.make_async_copy(own_src, dst, sems.at[0])
         tail = cache_src.at[pl.ds(cache_part - stretch_part, stretch_part), :]
-        from_cache = pltpu.make_async_copy(tail, dst, sems.at[0, i])
+        from_cache = pltpu.make_async_copy(tail, dst, sems.at[0])
         pl.when(last)(from_cache.start)
         pl.when(jnp.logical_not(last))(from_own.start)
-        copies.append(from_own)
-    for out, owner in ((2, 1 - sub_pos), (1, sub_pos)):
-        dst = (None, mine_ref, theirs_ref)[out]
-        at = pl.multiple_of(owner * kv_cols, HEAD_DIM) if split else 0
-        for i, (src, row, rows, col) in enumerate([
-            (k_ref, 0, stretch_part, 0),
-            (v_ref, 0, stretch_part, kv_cols),
-            (ck_ref, stretch_part, cache_part, 0),
-            (cv_ref, stretch_part, cache_part, kv_cols),
-        ]):
-            copy = pltpu.make_async_copy(
-                src.at[:, pl.ds(at, kv_cols)],
-                dst.at[pl.ds(row, rows), pl.ds(col, kv_cols)],
-                sems.at[out, i],
-            )
-            if i < 2:
+    cached = pl.ds(stretch_part, cache_part)
+    for n, (dst, owner) in enumerate([(theirs_ref, 1 - sub_pos), (mine_ref, sub_pos)]):
+        at = pl.multiple_of(owner * kv_cols, HEAD_DIM) if kv_cols != all_cols else 0
+        for src, rows, col, sem in [
+            (k_ref, pl.ds(0, stretch_part), 0, 0),
+            (v_ref, pl.ds(0, stretch_part), kv_cols, 0),
+            (ck_ref, cached, 0, 1 + n),
+            (cv_ref, cached, kv_cols, 1 + n),
+        ]:
+            part = src.at[:, pl.ds(at, kv_cols)]
+            copy = pltpu.make_async_copy(part, dst.at[rows, pl.ds(col, kv_cols)], sems.at[sem])
+            if sem:
+                pl.when(owns)(copy.start)
+            else:
                 copy.start()
-                copies.append(copy)
-            else:
-                pl.when(sends_cached)(copy.start)
-                cached.append(copy)
-    for copy in copies:
-        copy.wait()
-    for copy in cached:
-        pl.when(sends_cached)(copy.wait)
+
+    def wait_for(rows, sem):
+        pltpu.make_async_copy(mine_ref.at[rows, :], mine_ref.at[rows, :], sems.at[sem]).wait()
+
+    @pl.when(owns)
+    def _():
+        wait_for(cached, 1)
+        wait_for(cached, 2)
+
+    wait_for(pl.ds(0, stretch_part * (all_cols + 2 * kv_cols) // kv_cols), 0)
 
 
 def bias_kernel(prefix_len, stretch_part, cache_part, len_ref, bias_ref, lengths, sem):
@@ -145,7 +143,7 @@
 
 
 def later_kernel(picks, q_ref, bias_ref, max_ref, sum_ref, weighted_ref, *refs):
-    later_refs, (o_ref, out, sems) = refs[:-3], refs[-3:]
+    later_refs, (o_ref, out, sem) = refs[:-3], refs[-3:]
     ctx_pos, sub_pos = lax.axis_index("ctx"), lax.axis_index("sub")
     tok_rows, head_cols = q_ref.shape
     blocks = [None] * (bias_ref.shape[1] // tok_rows)
@@ -165,7 +163,6 @@
         for first in range(0, head_count, LATER_HEADS)
     ]
     attended = [attend(q_ref, bias, block, heads[0] // per_group, heads) for heads in batches]
-    copies = []
     for heads, (scores, values) in zip(batches, attended):
         old_max = stacked(max_ref, heads)
         row_max = jnp.maximum(old_max, jnp.max(scores, axis=1, keepdims=True))
@@ -179,11 +176,8 @@
             here = pl.ds(head * HEAD_DIM, HEAD_DIM)
             out[:, here] = result[i * tok_rows : (i + 1) * tok_rows]
         here = pl.ds(heads[0] * HEAD_DIM, len(heads) * HEAD_DIM)
-        copy = pltpu.make_async_copy(out.at[:, here], o_ref.at[:, here], sems.at[len(copies)])
-        copy.start()
-        copies.append(copy)
-    for copy in copies:
-        copy.wait()
+        pltpu.make_async_copy(out.at[:, here], o_ref.at[:, here], sem).start()
+    pltpu.make_async_copy(out, o_ref, sem).wait()
 
 
 def plan_rounds(n_ctx, n_sub, reach, tok_rows, cache_part, shard_rows):
@@ -237,16 +231,22 @@
         return [pltpu.with_memory_space_constraint(x, pltpu.HBM) for x in arrays]
 
     rounds = plan_rounds(n_ctx, n_sub, reach, tok_rows, cache_part, cache_part * n_sub)
-    first_sender = min(src for step in rounds for (src, _), leg in step.items() if leg[0] is not None)
+    owners = {
+        (source, row // cache_part)
+        for step in rounds
+        for (source, _), (first, _, _) in step.items()
+        if first is not None
+        for row in (first, first + tok_rows - 1)
+    }
     half = jax.ShapeDtypeStruct((stretch_part + cache_part, 2 * kv_cols), stretch_keys.dtype)
     raw, mine, theirs = pl.pallas_call(
-        functools.partial(pack_kernel, n_ctx, first_sender),
+        functools.partial(pack_kernel, n_ctx, sorted(owners)),
         out_shape=[
             jax.ShapeDtypeStruct((stretch_part, 2 * all_cols), stretch_keys.dtype), half, half
         ],
         in_specs=[hbm] * 4,
         out_specs=[vmem] * 3,
-        scratch_shapes=[pltpu.SemaphoreType.DMA((3, 4))],
+        scratch_shapes=[pltpu.SemaphoreType.DMA((3,))],
         compiler_params=small,
     )(*in_hbm(stretch_keys, stretch_values, cache_keys, cache_values))
     bias = pl.pallas_call(
@@ -295,7 +295,6 @@
         near_theirs = near
     far = swap_cores(near_theirs)
     mine_q = lax.dynamic_slice_in_dim(queries, sub_pos * head_cols, head_cols, 1)
-    head_count = head_cols // HEAD_DIM
     state = jax.ShapeDtypeStruct((tok_rows, head_cols), jnp.float32)
     large = pltpu.CompilerParams(vmem_limit_bytes=24 << 20)
     row_max, row_sum, weighted = pl.pallas_call(
@@ -312,7 +311,7 @@
         out_specs=hbm,
         scratch_shapes=[
             pltpu.VMEM((tok_rows, head_cols), queries.dtype),
-            pltpu.SemaphoreType.DMA((pl.cdiv(head_count, LATER_HEADS),)),
+            pltpu.SemaphoreType.DMA,
         ],
         compiler_params=large,
     )(mine_q, bias, row_max, row_sum, weighted, *later)

time: 16 us -> 15.6 us (0.975)
  waiting for transfers between devices: 2.14 us -> 1.89 us
    ppermute x2, starting transfers between devices: 5.63 us -> 5.35 us  [on_device(): later.append(lax.ppermute(block, ('ctx', 'sub'), pairs))]
    ppermute x2, starting transfers between devices: 2.15 us -> 2.44 us  [swap_cores(): return lax.ppermute(x, 'sub', [(0, 1), (1, 0)])]
    ppermute x2, waiting for transfers between devices: 2.03 us -> 1.78 us  [on_device(): later.append(lax.ppermute(block, ('ctx', 'sub'), pairs))]
where the time goes in v6:
time: 15.6 us; the launch traced here: 15.4 us
  starting transfers between devices  9.08 us (58%)
  Pallas kernels  4.18 us (27%)
  waiting for transfers between devices  1.89 us (12%)
    ppermute x2, starting transfers between devices, on_device(): later.append(lax.ppermute(block, ('ctx', 'sub'), pairs))  5.35 us
    ppermute x2, starting transfers between devices, swap_cores(): return lax.ppermute(x, 'sub', [(0, 1), (1, 0)])  2.44 us
    ppermute x2, waiting for transfers between devices, on_device(): later.append(lax.ppermute(block, ('ctx', 'sub'), pairs))  1.78 us
    pallas_call x1, Pallas kernels, on_device(): pl.pallas_call(functools.partial(later_kernel, picks), out_shape=jax.Shap...  1.53 us
    ppermute x1, starting transfers between devices, on_device(): lax.ppermute(raw, 'ctx', [(i, (i + 1) % n_ctx) for i in range(n_ctx)])  1.3 us
    pallas_call x1, Pallas kernels, on_device(): pl.pallas_call(functools.partial(pack_kernel, n_ctx, sorted(owners)), out...  0.98 us
    pallas_call x1, Pallas kernels, on_device(): pl.pallas_call(near_kernel, out_shape=[state] * 3, in_specs=[vmem] * 6, o...  0.91 us
    pallas_call x1, Pallas kernels, on_device(): pl.pallas_call(functools.partial(bias_kernel, prefix_len, stretch_part, c...  0.75 us
  transfers between devices with their start and end apart: 5, of which 3 were waited for; matrix products, arithmetic and copies ran while one was open for 1% of the time, Pallas kernels for 11%

profile of v6, /device:TPU:15, one launch (start us, length us, event | category | flops | bytes accessed | tf_op | source)
XLA Modules:
  0.0 15.4 jit_solution(9787504938617721792)
XLA Ops:
  0.0 0.0 copy-start
  0.0 1.0 %shard_map.65 = (bf16[64,1024]{1,0:T(8,128)(2,1)S(1)}, bf16[256,512]{1,0:T(8,128)(2,1)S(1)}, bf16[256,512]{1,0:T(8,128)(2,1)S(1)}) custom-call(bf16[64,512]{1,0:T(8,128)(2,1)} %k_ref.1, bf16[64,512]{1,0:T(8,128)(2,1)} %v_ref.1, bf16[192,512]{1,0:T(8,128)(2,1)} %ck_ref.1, bf16[192,512]{1,0:T(8,128)(2,1)} %cv_ref.1), custom_call_target="tpu_custom_call" | custom-call | tf_op jit(solution)/shard_map/pallas_call | solution.py:242
  1.0 0.7 %collective-permute-start = (bf16[256,512]{1,0:T(8,128)(2,1)S(1)}, bf16[256,512]{1,0:T(8,128)(2,1)S(1)}, u32[]{:S(2)}, u32[]{:S(2)}) collective-permute-start(bf16[256,512]{1,0:T(8,128)(2,1)S(1)} %get-tuple-element.13), channel_id=1, source_target_pairs={{0,1},{1,0},{2,3},{3,2},{4,5},{5,4},{6,7},{7,6},{8,9},{9,8},{10,11... | collective-permute-start | bytes 786440 | tf_op jit(solution)/shard_map/ppermute | solution.py:20
  1.7 1.3 %collective-permute-start.1 = (bf16[64,1024]{1,0:T(8,128)(2,1)S(1)}, bf16[64,1024]{1,0:T(8,128)(2,1)S(1)}, u32[]{:S(2)}, u32[]{:S(2)}) collective-permute-start(bf16[64,1024]{1,0:T(8,128)(2,1)S(1)} %get-tuple-element.14), channel_id=1, source_target_pairs={{0,4},{4,8},{8,12},{12,0},{1,5},{5,9},{9,13},{13,1},{2,6},{6,10},{... | collective-permute-start | bytes 393224 | tf_op jit(solution)/shard_map/ppermute | solution.py:262
  3.0 0.0 collective-permute-done.peer_ref
  3.1 0.1 fusion
  3.1 4.1 %collective-permute-start.3 = (bf16[128,512]{1,0:T(8,128)(2,1)S(1)}, bf16[128,512]{1,0:T(8,128)(2,1)S(1)}, u32[]{:S(2)}, u32[]{:S(2)}) collective-permute-start(bf16[128,512]{1,0:T(8,128)(2,1)S(1)} %get-tuple-element.19), channel_id=1, source_target_pairs={{12,0},{13,1},{0,8},{5,13},{14,2},{15,3},{2,10},{7,15},{28,16},{29... | collective-permute-start | bytes 393224 | tf_op jit(solution)/shard_map/ppermute | solution.py:281
  7.2 1.3 %collective-permute-start.4 = (bf16[128,512]{1,0:T(8,128)(2,1)S(1)}, bf16[128,512]{1,0:T(8,128)(2,1)S(1)}, u32[]{:S(2)}, u32[]{:S(2)}) collective-permute-start(bf16[128,512]{1,0:T(8,128)(2,1)S(1)} %get-tuple-element.20), channel_id=1, source_target_pairs={{12,4},{13,5},{1,9},{4,12},{14,6},{15,7},{3,11},{6,14},{28,20},{29... | collective-permute-start | bytes 393224 | tf_op jit(solution)/shard_map/ppermute | solution.py:281
  8.5 0.0 collective-permute-done.1.near_ref
  8.6 1.7 %collective-permute-start.2 = (bf16[64,512]{1,0:T(8,128)(2,1)S(1)}, bf16[64,512]{1,0:T(8,128)(2,1)S(1)}, u32[]{:S(2)}, u32[]{:S(2)}) collective-permute-start(bf16[64,512]{1,0:T(8,128)(2,1)S(1)} %pad_maximum_fusion.1), channel_id=1, source_target_pairs={{0,1},{1,0},{2,3},{3,2},{4,5},{5,4},{6,7},{7,6},{8,9},{9,8},{10,11... | collective-permute-start | bytes 196616 | tf_op jit(solution)/shard_map/ppermute | solution.py:20
  10.3 0.0 copy-done
  10.3 0.8 %shard_map.64.bias_ref = f32[128,384]{1,0:T(8,128)S(1)} custom-call(s32[12]{0:T(128)} %len_ref.1), custom_call_target="tpu_custom_call" | custom-call | tf_op jit(solution)/shard_map/pallas_call | solution.py:252
  11.1 0.1 collective-permute-done.2.far_ref
  11.2 0.9 %shard_map.66 = (f32[128,2048]{1,0:T(8,128)S(1)}, f32[128,2048]{1,0:T(8,128)S(1)}, f32[128,2048]{1,0:T(8,128)S(1)}) custom-call(bf16[128,2048]{1,0:T(8,128)(2,1)S(1)} %constant_dynamic-slice_fusion.2.q_ref, f32[128,384]{1,0:T(8,128)S(1)} %shard_map.64.bias_ref, bf16[256,512]{1,0:T(8,128)(2,1)S(1)} %get-tuple-element.12.own_ref, ...), custom_call_target="tpu_custom_call" | custom-call | tf_op jit(solution)/shard_map/pallas_call | solution.py:300
  12.1 0.3 %collective-permute-done.3.refs_0_ = bf16[128,512]{1,0:T(8,128)(2,1)S(1)} collective-permute-done((bf16[128,512]{1,0:T(8,128)(2,1)S(1)}, bf16[128,512]{1,0:T(8,128)(2,1)S(1)}, u32[]{:S(2)}, u32[]{:S(2)}) %collective-permute-start.3) | collective-permute-done | bytes 131104 | tf_op jit(solution)/shard_map/ppermute | solution.py:281
  12.4 1.4 %collective-permute-done.4.refs_1_ = bf16[128,512]{1,0:T(8,128)(2,1)S(1)} collective-permute-done((bf16[128,512]{1,0:T(8,128)(2,1)S(1)}, bf16[128,512]{1,0:T(8,128)(2,1)S(1)}, u32[]{:S(2)}, u32[]{:S(2)}) %collective-permute-start.4) | collective-permute-done | bytes 131104 | tf_op jit(solution)/shard_map/ppermute | solution.py:281
  13.9 1.5 %shard_map.67 = bf16[128,2048]{1,0:T(8,128)(2,1)} custom-call(bf16[128,2048]{1,0:T(8,128)(2,1)S(1)} %constant_dynamic-slice_fusion.2.q_ref, f32[128,384]{1,0:T(8,128)S(1)} %shard_map.64.bias_ref, f32[128,2048]{1,0:T(8,128)S(1)} %get-tuple-element.16.max_ref, f32[128,2048]{1,0:T(8,128)S(1)} %get-tuple-element.17.sum_ref, ...), custom_call_target="tpu_custom_call" | custom-call | tf_op jit(solution)/shard_map/pallas_call | solution.py:307
  (5 shorter events, 0.1 us)
Async XLA Ops:
  0.0 10.3 %copy-start = (bf16[128,4096]{1,0:T(8,128)(2,1)S(1)}, bf16[128,4096]{1,0:T(8,128)(2,1)}, u32[]{:S(2)}) copy-start(bf16[128,4096]{1,0:T(8,128)(2,1)} %param.6) | copy-start | bytes 3145732
  1.0 2.0 %collective-permute-start = (bf16[256,512]{1,0:T(8,128)(2,1)S(1)}, bf16[256,512]{1,0:T(8,128)(2,1)S(1)}, u32[]{:S(2)}, u32[]{:S(2)}) collective-permute-start(bf16[256,512]{1,0:T(8,128)(2,1)S(1)} %get-tuple-element.13), channel_id=1, source_target_pairs={{0,1},{1,0},{2,3},{3,2},{4,5},{5,4},{6,7},{7,6},{8,9},{9,8},{10,11... | collective-permute-start | bytes 786440 | tf_op jit(solution)/shard_map/ppermute | solution.py:20
  1.7 6.8 %collective-permute-start.1 = (bf16[64,1024]{1,0:T(8,128)(2,1)S(1)}, bf16[64,1024]{1,0:T(8,128)(2,1)S(1)}, u32[]{:S(2)}, u32[]{:S(2)}) collective-permute-start(bf16[64,1024]{1,0:T(8,128)(2,1)S(1)} %get-tuple-element.14), channel_id=1, source_target_pairs={{0,4},{4,8},{8,12},{12,0},{1,5},{5,9},{9,13},{13,1},{2,6},{6,10},{... | collective-permute-start | bytes 393224 | tf_op jit(solution)/shard_map/ppermute | solution.py:262
  3.1 9.3 %collective-permute-start.3 = (bf16[128,512]{1,0:T(8,128)(2,1)S(1)}, bf16[128,512]{1,0:T(8,128)(2,1)S(1)}, u32[]{:S(2)}, u32[]{:S(2)}) collective-permute-start(bf16[128,512]{1,0:T(8,128)(2,1)S(1)} %get-tuple-element.19), channel_id=1, source_target_pairs={{12,0},{13,1},{0,8},{5,13},{14,2},{15,3},{2,10},{7,15},{28,16},{29... | collective-permute-start | bytes 393224 | tf_op jit(solution)/shard_map/ppermute | solution.py:281
  7.2 6.6 %collective-permute-start.4 = (bf16[128,512]{1,0:T(8,128)(2,1)S(1)}, bf16[128,512]{1,0:T(8,128)(2,1)S(1)}, u32[]{:S(2)}, u32[]{:S(2)}) collective-permute-start(bf16[128,512]{1,0:T(8,128)(2,1)S(1)} %get-tuple-element.20), channel_id=1, source_target_pairs={{12,4},{13,5},{1,9},{4,12},{14,6},{15,7},{3,11},{6,14},{28,20},{29... | collective-permute-start | bytes 393224 | tf_op jit(solution)/shard_map/ppermute | solution.py:281
  8.6 2.6 %collective-permute-start.2 = (bf16[64,512]{1,0:T(8,128)(2,1)S(1)}, bf16[64,512]{1,0:T(8,128)(2,1)S(1)}, u32[]{:S(2)}, u32[]{:S(2)}) collective-permute-start(bf16[64,512]{1,0:T(8,128)(2,1)S(1)} %pad_maximum_fusion.1), channel_id=1, source_target_pairs={{0,1},{1,0},{2,3},{3,2},{4,5},{5,4},{6,7},{7,6},{8,9},{9,8},{10,11... | collective-permute-start | bytes 196616 | tf_op jit(solution)/shard_map/ppermute | solution.py:20

commit v7 on v6

--- a/solution.py
+++ b/solution.py
@@ -202,7 +202,8 @@
                 i for i, step in enumerate(rounds)
                 if (source, sub) not in step and (dest, sub) not in dests[i]
             ]
-            free.sort(key=lambda i: ((source, sub) in dests[i]) == (sub > 0))
+            if sub == 0:
+                free.sort(key=lambda i: (source, sub) not in dests[i])
             if not free:
                 rounds.append({})
                 free = [len(rounds) - 1]

time: 15.6 us -> 15.6 us (level)
  no operation moved by 1% of the time
where the time goes in v7:
time: 15.6 us; the launch traced here: 15.4 us
  starting transfers between devices  9.08 us (58%)
  Pallas kernels  4.17 us (27%)
  waiting for transfers between devices  1.89 us (12%)
    ppermute x2, starting transfers between devices, on_device(): later.append(lax.ppermute(block, ('ctx', 'sub'), pairs))  5.35 us
    ppermute x2, starting transfers between devices, swap_cores(): return lax.ppermute(x, 'sub', [(0, 1), (1, 0)])  2.44 us
    ppermute x2, waiting for transfers between devices, on_device(): later.append(lax.ppermute(block, ('ctx', 'sub'), pairs))  1.78 us
    pallas_call x1, Pallas kernels, on_device(): pl.pallas_call(functools.partial(later_kernel, picks), out_shape=jax.Shap...  1.52 us
    ppermute x1, starting transfers between devices, on_device(): lax.ppermute(raw, 'ctx', [(i, (i + 1) % n_ctx) for i in range(n_ctx)])  1.3 us
    pallas_call x1, Pallas kernels, on_device(): pl.pallas_call(functools.partial(pack_kernel, n_ctx, sorted(owners)), out...  0.98 us
    pallas_call x1, Pallas kernels, on_device(): pl.pallas_call(near_kernel, out_shape=[state] * 3, in_specs=[vmem] * 6, o...  0.91 us
    pallas_call x1, Pallas kernels, on_device(): pl.pallas_call(functools.partial(bias_kernel, prefix_len, stretch_part, c...  0.75 us
  transfers between devices with their start and end apart: 5, of which 3 were waited for; matrix products, arithmetic and copies ran while one was open for 1% of the time, Pallas kernels for 11%

profile of v7, /device:TPU:15, one launch (start us, length us, event | category | flops | bytes accessed | tf_op | source)
XLA Modules:
  0.0 15.4 jit_solution(11044712307764272158)
XLA Ops:
  0.0 0.0 copy-start
  0.0 1.0 %shard_map.65 = (bf16[64,1024]{1,0:T(8,128)(2,1)S(1)}, bf16[256,512]{1,0:T(8,128)(2,1)S(1)}, bf16[256,512]{1,0:T(8,128)(2,1)S(1)}) custom-call(bf16[64,512]{1,0:T(8,128)(2,1)} %k_ref.1, bf16[64,512]{1,0:T(8,128)(2,1)} %v_ref.1, bf16[192,512]{1,0:T(8,128)(2,1)} %ck_ref.1, bf16[192,512]{1,0:T(8,128)(2,1)} %cv_ref.1), custom_call_target="tpu_custom_call" | custom-call | tf_op jit(solution)/shard_map/pallas_call | solution.py:243
  1.0 0.7 %collective-permute-start = (bf16[256,512]{1,0:T(8,128)(2,1)S(1)}, bf16[256,512]{1,0:T(8,128)(2,1)S(1)}, u32[]{:S(2)}, u32[]{:S(2)}) collective-permute-start(bf16[256,512]{1,0:T(8,128)(2,1)S(1)} %get-tuple-element.13), channel_id=1, source_target_pairs={{0,1},{1,0},{2,3},{3,2},{4,5},{5,4},{6,7},{7,6},{8,9},{9,8},{10,11... | collective-permute-start | bytes 786440 | tf_op jit(solution)/shard_map/ppermute | solution.py:20
  1.7 1.3 %collective-permute-start.1 = (bf16[64,1024]{1,0:T(8,128)(2,1)S(1)}, bf16[64,1024]{1,0:T(8,128)(2,1)S(1)}, u32[]{:S(2)}, u32[]{:S(2)}) collective-permute-start(bf16[64,1024]{1,0:T(8,128)(2,1)S(1)} %get-tuple-element.14), channel_id=1, source_target_pairs={{0,4},{4,8},{8,12},{12,0},{1,5},{5,9},{9,13},{13,1},{2,6},{6,10},{... | collective-permute-start | bytes 393224 | tf_op jit(solution)/shard_map/ppermute | solution.py:263
  3.0 0.0 collective-permute-done.peer_ref
  3.1 0.1 fusion
  3.1 4.1 %collective-permute-start.3 = (bf16[128,512]{1,0:T(8,128)(2,1)S(1)}, bf16[128,512]{1,0:T(8,128)(2,1)S(1)}, u32[]{:S(2)}, u32[]{:S(2)}) collective-permute-start(bf16[128,512]{1,0:T(8,128)(2,1)S(1)} %get-tuple-element.19), channel_id=1, source_target_pairs={{12,0},{13,1},{0,8},{1,9},{5,13},{14,2},{15,3},{2,10},{3,11},{7,15... | collective-permute-start | bytes 393224 | tf_op jit(solution)/shard_map/ppermute | solution.py:282
  7.2 1.3 %collective-permute-start.4 = (bf16[128,512]{1,0:T(8,128)(2,1)S(1)}, bf16[128,512]{1,0:T(8,128)(2,1)S(1)}, u32[]{:S(2)}, u32[]{:S(2)}) collective-permute-start(bf16[128,512]{1,0:T(8,128)(2,1)S(1)} %get-tuple-element.20), channel_id=1, source_target_pairs={{12,4},{13,5},{4,12},{14,6},{15,7},{6,14},{28,20},{29,21},{20,28},... | collective-permute-start | bytes 393224 | tf_op jit(solution)/shard_map/ppermute | solution.py:282
  8.5 0.0 collective-permute-done.1.near_ref
  8.6 1.7 %collective-permute-start.2 = (bf16[64,512]{1,0:T(8,128)(2,1)S(1)}, bf16[64,512]{1,0:T(8,128)(2,1)S(1)}, u32[]{:S(2)}, u32[]{:S(2)}) collective-permute-start(bf16[64,512]{1,0:T(8,128)(2,1)S(1)} %pad_maximum_fusion.1), channel_id=1, source_target_pairs={{0,1},{1,0},{2,3},{3,2},{4,5},{5,4},{6,7},{7,6},{8,9},{9,8},{10,11... | collective-permute-start | bytes 196616 | tf_op jit(solution)/shard_map/ppermute | solution.py:20
  10.3 0.0 copy-done
  10.3 0.8 %shard_map.64.bias_ref = f32[128,384]{1,0:T(8,128)S(1)} custom-call(s32[12]{0:T(128)} %len_ref.1), custom_call_target="tpu_custom_call" | custom-call | tf_op jit(solution)/shard_map/pallas_call | solution.py:253
  11.1 0.1 collective-permute-done.2.far_ref
  11.2 0.9 %shard_map.66 = (f32[128,2048]{1,0:T(8,128)S(1)}, f32[128,2048]{1,0:T(8,128)S(1)}, f32[128,2048]{1,0:T(8,128)S(1)}) custom-call(bf16[128,2048]{1,0:T(8,128)(2,1)S(1)} %constant_dynamic-slice_fusion.2.q_ref, f32[128,384]{1,0:T(8,128)S(1)} %shard_map.64.bias_ref, bf16[256,512]{1,0:T(8,128)(2,1)S(1)} %get-tuple-element.12.own_ref, ...), custom_call_target="tpu_custom_call" | custom-call | tf_op jit(solution)/shard_map/pallas_call | solution.py:301
  12.1 0.9 %collective-permute-done.3.refs_0_ = bf16[128,512]{1,0:T(8,128)(2,1)S(1)} collective-permute-done((bf16[128,512]{1,0:T(8,128)(2,1)S(1)}, bf16[128,512]{1,0:T(8,128)(2,1)S(1)}, u32[]{:S(2)}, u32[]{:S(2)}) %collective-permute-start.3) | collective-permute-done | bytes 131104 | tf_op jit(solution)/shard_map/ppermute | solution.py:282
  13.0 0.9 %collective-permute-done.4.refs_1_ = bf16[128,512]{1,0:T(8,128)(2,1)S(1)} collective-permute-done((bf16[128,512]{1,0:T(8,128)(2,1)S(1)}, bf16[128,512]{1,0:T(8,128)(2,1)S(1)}, u32[]{:S(2)}, u32[]{:S(2)}) %collective-permute-start.4) | collective-permute-done | bytes 131104 | tf_op jit(solution)/shard_map/ppermute | solution.py:282
  13.9 1.5 %shard_map.67 = bf16[128,2048]{1,0:T(8,128)(2,1)} custom-call(bf16[128,2048]{1,0:T(8,128)(2,1)S(1)} %constant_dynamic-slice_fusion.2.q_ref, f32[128,384]{1,0:T(8,128)S(1)} %shard_map.64.bias_ref, f32[128,2048]{1,0:T(8,128)S(1)} %get-tuple-element.16.max_ref, f32[128,2048]{1,0:T(8,128)S(1)} %get-tuple-element.17.sum_ref, ...), custom_call_target="tpu_custom_call" | custom-call | tf_op jit(solution)/shard_map/pallas_call | solution.py:308
  (5 shorter events, 0.1 us)
Async XLA Ops:
  0.0 10.3 %copy-start = (bf16[128,4096]{1,0:T(8,128)(2,1)S(1)}, bf16[128,4096]{1,0:T(8,128)(2,1)}, u32[]{:S(2)}) copy-start(bf16[128,4096]{1,0:T(8,128)(2,1)} %param.6) | copy-start | bytes 3145732
  1.0 2.0 %collective-permute-start = (bf16[256,512]{1,0:T(8,128)(2,1)S(1)}, bf16[256,512]{1,0:T(8,128)(2,1)S(1)}, u32[]{:S(2)}, u32[]{:S(2)}) collective-permute-start(bf16[256,512]{1,0:T(8,128)(2,1)S(1)} %get-tuple-element.13), channel_id=1, source_target_pairs={{0,1},{1,0},{2,3},{3,2},{4,5},{5,4},{6,7},{7,6},{8,9},{9,8},{10,11... | collective-permute-start | bytes 786440 | tf_op jit(solution)/shard_map/ppermute | solution.py:20
  1.7 6.8 %collective-permute-start.1 = (bf16[64,1024]{1,0:T(8,128)(2,1)S(1)}, bf16[64,1024]{1,0:T(8,128)(2,1)S(1)}, u32[]{:S(2)}, u32[]{:S(2)}) collective-permute-start(bf16[64,1024]{1,0:T(8,128)(2,1)S(1)} %get-tuple-element.14), channel_id=1, source_target_pairs={{0,4},{4,8},{8,12},{12,0},{1,5},{5,9},{9,13},{13,1},{2,6},{6,10},{... | collective-permute-start | bytes 393224 | tf_op jit(solution)/shard_map/ppermute | solution.py:263
  3.1 9.9 %collective-permute-start.3 = (bf16[128,512]{1,0:T(8,128)(2,1)S(1)}, bf16[128,512]{1,0:T(8,128)(2,1)S(1)}, u32[]{:S(2)}, u32[]{:S(2)}) collective-permute-start(bf16[128,512]{1,0:T(8,128)(2,1)S(1)} %get-tuple-element.19), channel_id=1, source_target_pairs={{12,0},{13,1},{0,8},{1,9},{5,13},{14,2},{15,3},{2,10},{3,11},{7,15... | collective-permute-start | bytes 393224 | tf_op jit(solution)/shard_map/ppermute | solution.py:282
  7.2 6.6 %collective-permute-start.4 = (bf16[128,512]{1,0:T(8,128)(2,1)S(1)}, bf16[128,512]{1,0:T(8,128)(2,1)S(1)}, u32[]{:S(2)}, u32[]{:S(2)}) collective-permute-start(bf16[128,512]{1,0:T(8,128)(2,1)S(1)} %get-tuple-element.20), channel_id=1, source_target_pairs={{12,4},{13,5},{4,12},{14,6},{15,7},{6,14},{28,20},{29,21},{20,28},... | collective-permute-start | bytes 393224 | tf_op jit(solution)/shard_map/ppermute | solution.py:282
  8.6 2.6 %collective-permute-start.2 = (bf16[64,512]{1,0:T(8,128)(2,1)S(1)}, bf16[64,512]{1,0:T(8,128)(2,1)S(1)}, u32[]{:S(2)}, u32[]{:S(2)}) collective-permute-start(bf16[64,512]{1,0:T(8,128)(2,1)S(1)} %pad_maximum_fusion.1), channel_id=1, source_target_pairs={{0,1},{1,0},{2,3},{3,2},{4,5},{5,4},{6,7},{7,6},{8,9},{9,8},{10,11... | collective-permute-start | bytes 196616 | tf_op jit(solution)/shard_map/ppermute | solution.py:20

commit v8 on v6

--- a/solution.py
+++ b/solution.py
@@ -14,6 +14,7 @@
 EXP2_SCALE = SCORE_SCALE * math.log2(math.e)
 HEADS_AT_ONCE = 8
 LATER_HEADS = 2
+HEADS_PER_COPY = 4
 
 
 def swap_cores(x):
@@ -175,8 +176,11 @@
         for i, head in enumerate(heads):
             here = pl.ds(head * HEAD_DIM, HEAD_DIM)
             out[:, here] = result[i * tok_rows : (i + 1) * tok_rows]
-        here = pl.ds(heads[0] * HEAD_DIM, len(heads) * HEAD_DIM)
-        pltpu.make_async_copy(out.at[:, here], o_ref.at[:, here], sem).start()
+        done = heads[-1] + 1
+        if done % HEADS_PER_COPY == 0 or done == head_count:
+            at = (done - 1) // HEADS_PER_COPY * HEADS_PER_COPY
+            here = pl.ds(at * HEAD_DIM, (done - at) * HEAD_DIM)
+            pltpu.make_async_copy(out.at[:, here], o_ref.at[:, here], sem).start()
     pltpu.make_async_copy(out, o_ref, sem).wait()
 
 

time: 15.6 us -> 15.5 us (level)
  no operation moved by 1% of the time
where the time goes in v8:
time: 15.5 us; the launch traced here: 15.4 us
  starting transfers between devices  9.08 us (59%)
  Pallas kernels  4.15 us (27%)
  waiting for transfers between devices  1.89 us (12%)
    ppermute x2, starting transfers between devices, on_device(): later.append(lax.ppermute(block, ('ctx', 'sub'), pairs))  5.35 us
    ppermute x2, starting transfers between devices, swap_cores(): return lax.ppermute(x, 'sub', [(0, 1), (1, 0)])  2.44 us
    ppermute x2, waiting for transfers between devices, on_device(): later.append(lax.ppermute(block, ('ctx', 'sub'), pairs))  1.78 us
    pallas_call x1, Pallas kernels, on_device(): pl.pallas_call(functools.partial(later_kernel, picks), out_shape=jax.Shap...  1.5 us
    ppermute x1, starting transfers between devices, on_device(): lax.ppermute(raw, 'ctx', [(i, (i + 1) % n_ctx) for i in range(n_ctx)])  1.3 us
    pallas_call x1, Pallas kernels, on_device(): pl.pallas_call(functools.partial(pack_kernel, n_ctx, sorted(owners)), out...  0.98 us
    pallas_call x1, Pallas kernels, on_device(): pl.pallas_call(near_kernel, out_shape=[state] * 3, in_specs=[vmem] * 6, o...  0.91 us
    pallas_call x1, Pallas kernels, on_device(): pl.pallas_call(functools.partial(bias_kernel, prefix_len, stretch_part, c...  0.75 us
  transfers between devices with their start and end apart: 5, of which 3 were waited for; matrix products, arithmetic and copies ran while one was open for 1% of the time, Pallas kernels for 11%

profile of v8, /device:TPU:15, one launch (start us, length us, event | category | flops | bytes accessed | tf_op | source)
XLA Modules:
  0.0 15.4 jit_solution(5304310536547420705)
XLA Ops:
  0.0 0.0 copy-start
  0.0 1.0 %shard_map.65 = (bf16[64,1024]{1,0:T(8,128)(2,1)S(1)}, bf16[256,512]{1,0:T(8,128)(2,1)S(1)}, bf16[256,512]{1,0:T(8,128)(2,1)S(1)}) custom-call(bf16[64,512]{1,0:T(8,128)(2,1)} %k_ref.1, bf16[64,512]{1,0:T(8,128)(2,1)} %v_ref.1, bf16[192,512]{1,0:T(8,128)(2,1)} %ck_ref.1, bf16[192,512]{1,0:T(8,128)(2,1)} %cv_ref.1), custom_call_target="tpu_custom_call" | custom-call | tf_op jit(solution)/shard_map/pallas_call | solution.py:246
  1.0 0.7 %collective-permute-start = (bf16[256,512]{1,0:T(8,128)(2,1)S(1)}, bf16[256,512]{1,0:T(8,128)(2,1)S(1)}, u32[]{:S(2)}, u32[]{:S(2)}) collective-permute-start(bf16[256,512]{1,0:T(8,128)(2,1)S(1)} %get-tuple-element.13), channel_id=1, source_target_pairs={{0,1},{1,0},{2,3},{3,2},{4,5},{5,4},{6,7},{7,6},{8,9},{9,8},{10,11... | collective-permute-start | bytes 786440 | tf_op jit(solution)/shard_map/ppermute | solution.py:21
  1.7 1.3 %collective-permute-start.1 = (bf16[64,1024]{1,0:T(8,128)(2,1)S(1)}, bf16[64,1024]{1,0:T(8,128)(2,1)S(1)}, u32[]{:S(2)}, u32[]{:S(2)}) collective-permute-start(bf16[64,1024]{1,0:T(8,128)(2,1)S(1)} %get-tuple-element.14), channel_id=1, source_target_pairs={{0,4},{4,8},{8,12},{12,0},{1,5},{5,9},{9,13},{13,1},{2,6},{6,10},{... | collective-permute-start | bytes 393224 | tf_op jit(solution)/shard_map/ppermute | solution.py:266
  3.0 0.0 collective-permute-done.peer_ref
  3.1 0.1 fusion
  3.1 4.1 %collective-permute-start.3 = (bf16[128,512]{1,0:T(8,128)(2,1)S(1)}, bf16[128,512]{1,0:T(8,128)(2,1)S(1)}, u32[]{:S(2)}, u32[]{:S(2)}) collective-permute-start(bf16[128,512]{1,0:T(8,128)(2,1)S(1)} %get-tuple-element.19), channel_id=1, source_target_pairs={{12,0},{13,1},{0,8},{5,13},{14,2},{15,3},{2,10},{7,15},{28,16},{29... | collective-permute-start | bytes 393224 | tf_op jit(solution)/shard_map/ppermute | solution.py:285
  7.2 1.3 %collective-permute-start.4 = (bf16[128,512]{1,0:T(8,128)(2,1)S(1)}, bf16[128,512]{1,0:T(8,128)(2,1)S(1)}, u32[]{:S(2)}, u32[]{:S(2)}) collective-permute-start(bf16[128,512]{1,0:T(8,128)(2,1)S(1)} %get-tuple-element.20), channel_id=1, source_target_pairs={{12,4},{13,5},{1,9},{4,12},{14,6},{15,7},{3,11},{6,14},{28,20},{29... | collective-permute-start | bytes 393224 | tf_op jit(solution)/shard_map/ppermute | solution.py:285
  8.5 0.0 collective-permute-done.1.near_ref
  8.6 1.7 %collective-permute-start.2 = (bf16[64,512]{1,0:T(8,128)(2,1)S(1)}, bf16[64,512]{1,0:T(8,128)(2,1)S(1)}, u32[]{:S(2)}, u32[]{:S(2)}) collective-permute-start(bf16[64,512]{1,0:T(8,128)(2,1)S(1)} %pad_maximum_fusion.1), channel_id=1, source_target_pairs={{0,1},{1,0},{2,3},{3,2},{4,5},{5,4},{6,7},{7,6},{8,9},{9,8},{10,11... | collective-permute-start | bytes 196616 | tf_op jit(solution)/shard_map/ppermute | solution.py:21
  10.3 0.0 copy-done
  10.3 0.8 %shard_map.64.bias_ref = f32[128,384]{1,0:T(8,128)S(1)} custom-call(s32[12]{0:T(128)} %len_ref.1), custom_call_target="tpu_custom_call" | custom-call | tf_op jit(solution)/shard_map/pallas_call | solution.py:256
  11.1 0.1 collective-permute-done.2.far_ref
  11.2 0.9 %shard_map.66 = (f32[128,2048]{1,0:T(8,128)S(1)}, f32[128,2048]{1,0:T(8,128)S(1)}, f32[128,2048]{1,0:T(8,128)S(1)}) custom-call(bf16[128,2048]{1,0:T(8,128)(2,1)S(1)} %constant_dynamic-slice_fusion.2.q_ref, f32[128,384]{1,0:T(8,128)S(1)} %shard_map.64.bias_ref, bf16[256,512]{1,0:T(8,128)(2,1)S(1)} %get-tuple-element.12.own_ref, ...), custom_call_target="tpu_custom_call" | custom-call | tf_op jit(solution)/shard_map/pallas_call | solution.py:304
  12.1 0.3 %collective-permute-done.3.refs_0_ = bf16[128,512]{1,0:T(8,128)(2,1)S(1)} collective-permute-done((bf16[128,512]{1,0:T(8,128)(2,1)S(1)}, bf16[128,512]{1,0:T(8,128)(2,1)S(1)}, u32[]{:S(2)}, u32[]{:S(2)}) %collective-permute-start.3) | collective-permute-done | bytes 131104 | tf_op jit(solution)/shard_map/ppermute | solution.py:285
  12.4 1.4 %collective-permute-done.4.refs_1_ = bf16[128,512]{1,0:T(8,128)(2,1)S(1)} collective-permute-done((bf16[128,512]{1,0:T(8,128)(2,1)S(1)}, bf16[128,512]{1,0:T(8,128)(2,1)S(1)}, u32[]{:S(2)}, u32[]{:S(2)}) %collective-permute-start.4) | collective-permute-done | bytes 131104 | tf_op jit(solution)/shard_map/ppermute | solution.py:285
  13.9 1.5 %shard_map.67 = bf16[128,2048]{1,0:T(8,128)(2,1)} custom-call(bf16[128,2048]{1,0:T(8,128)(2,1)S(1)} %constant_dynamic-slice_fusion.2.q_ref, f32[128,384]{1,0:T(8,128)S(1)} %shard_map.64.bias_ref, f32[128,2048]{1,0:T(8,128)S(1)} %get-tuple-element.16.max_ref, f32[128,2048]{1,0:T(8,128)S(1)} %get-tuple-element.17.sum_ref, ...), custom_call_target="tpu_custom_call" | custom-call | tf_op jit(solution)/shard_map/pallas_call | solution.py:311
  (5 shorter events, 0.1 us)
Async XLA Ops:
  0.0 10.3 %copy-start = (bf16[128,4096]{1,0:T(8,128)(2,1)S(1)}, bf16[128,4096]{1,0:T(8,128)(2,1)}, u32[]{:S(2)}) copy-start(bf16[128,4096]{1,0:T(8,128)(2,1)} %param.6) | copy-start | bytes 3145732
  1.0 2.0 %collective-permute-start = (bf16[256,512]{1,0:T(8,128)(2,1)S(1)}, bf16[256,512]{1,0:T(8,128)(2,1)S(1)}, u32[]{:S(2)}, u32[]{:S(2)}) collective-permute-start(bf16[256,512]{1,0:T(8,128)(2,1)S(1)} %get-tuple-element.13), channel_id=1, source_target_pairs={{0,1},{1,0},{2,3},{3,2},{4,5},{5,4},{6,7},{7,6},{8,9},{9,8},{10,11... | collective-permute-start | bytes 786440 | tf_op jit(solution)/shard_map/ppermute | solution.py:21
  1.7 6.8 %collective-permute-start.1 = (bf16[64,1024]{1,0:T(8,128)(2,1)S(1)}, bf16[64,1024]{1,0:T(8,128)(2,1)S(1)}, u32[]{:S(2)}, u32[]{:S(2)}) collective-permute-start(bf16[64,1024]{1,0:T(8,128)(2,1)S(1)} %get-tuple-element.14), channel_id=1, source_target_pairs={{0,4},{4,8},{8,12},{12,0},{1,5},{5,9},{9,13},{13,1},{2,6},{6,10},{... | collective-permute-start | bytes 393224 | tf_op jit(solution)/shard_map/ppermute | solution.py:266
  3.1 9.3 %collective-permute-start.3 = (bf16[128,512]{1,0:T(8,128)(2,1)S(1)}, bf16[128,512]{1,0:T(8,128)(2,1)S(1)}, u32[]{:S(2)}, u32[]{:S(2)}) collective-permute-start(bf16[128,512]{1,0:T(8,128)(2,1)S(1)} %get-tuple-element.19), channel_id=1, source_target_pairs={{12,0},{13,1},{0,8},{5,13},{14,2},{15,3},{2,10},{7,15},{28,16},{29... | collective-permute-start | bytes 393224 | tf_op jit(solution)/shard_map/ppermute | solution.py:285
  7.2 6.6 %collective-permute-start.4 = (bf16[128,512]{1,0:T(8,128)(2,1)S(1)}, bf16[128,512]{1,0:T(8,128)(2,1)S(1)}, u32[]{:S(2)}, u32[]{:S(2)}) collective-permute-start(bf16[128,512]{1,0:T(8,128)(2,1)S(1)} %get-tuple-element.20), channel_id=1, source_target_pairs={{12,4},{13,5},{1,9},{4,12},{14,6},{15,7},{3,11},{6,14},{28,20},{29... | collective-permute-start | bytes 393224 | tf_op jit(solution)/shard_map/ppermute | solution.py:285
  8.6 2.6 %collective-permute-start.2 = (bf16[64,512]{1,0:T(8,128)(2,1)S(1)}, bf16[64,512]{1,0:T(8,128)(2,1)S(1)}, u32[]{:S(2)}, u32[]{:S(2)}) collective-permute-start(bf16[64,512]{1,0:T(8,128)(2,1)S(1)} %pad_maximum_fusion.1), channel_id=1, source_target_pairs={{0,1},{1,0},{2,3},{3,2},{4,5},{5,4},{6,7},{7,6},{8,9},{9,8},{10,11... | collective-permute-start | bytes 196616 | tf_op jit(solution)/shard_map/ppermute | solution.py:21

commit v9 on v6

--- a/solution.py
+++ b/solution.py
@@ -38,10 +38,10 @@
     for n, (dst, owner) in enumerate([(theirs_ref, 1 - sub_pos), (mine_ref, sub_pos)]):
         at = pl.multiple_of(owner * kv_cols, HEAD_DIM) if kv_cols != all_cols else 0
         for src, rows, col, sem in [
+            (ck_ref, cached, 0, 1 + n),
+            (cv_ref, cached, kv_cols, 1 + n),
             (k_ref, pl.ds(0, stretch_part), 0, 0),
             (v_ref, pl.ds(0, stretch_part), kv_cols, 0),
-            (ck_ref, cached, 0, 1 + n),
-            (cv_ref, cached, kv_cols, 1 + n),
         ]:
             part = src.at[:, pl.ds(at, kv_cols)]
             copy = pltpu.make_async_copy(part, dst.at[rows, pl.ds(col, kv_cols)], sems.at[sem])

time: 15.6 us -> 15.6 us (level)
  no operation moved by 1% of the time
where the time goes in v9:
time: 15.6 us; the launch traced here: 15.4 us
  starting transfers between devices  9.08 us (58%)
  Pallas kernels  4.18 us (27%)
  waiting for transfers between devices  1.89 us (12%)
    ppermute x2, starting transfers between devices, on_device(): later.append(lax.ppermute(block, ('ctx', 'sub'), pairs))  5.35 us
    ppermute x2, starting transfers between devices, swap_cores(): return lax.ppermute(x, 'sub', [(0, 1), (1, 0)])  2.44 us
    ppermute x2, waiting for transfers between devices, on_device(): later.append(lax.ppermute(block, ('ctx', 'sub'), pairs))  1.78 us
    pallas_call x1, Pallas kernels, on_device(): pl.pallas_call(functools.partial(later_kernel, picks), out_shape=jax.Shap...  1.53 us
    ppermute x1, starting transfers between devices, on_device(): lax.ppermute(raw, 'ctx', [(i, (i + 1) % n_ctx) for i in range(n_ctx)])  1.3 us
    pallas_call x1, Pallas kernels, on_device(): pl.pallas_call(functools.partial(pack_kernel, n_ctx, sorted(owners)), out...  0.98 us
    pallas_call x1, Pallas kernels, on_device(): pl.pallas_call(near_kernel, out_shape=[state] * 3, in_specs=[vmem] * 6, o...  0.91 us
    pallas_call x1, Pallas kernels, on_device(): pl.pallas_call(functools.partial(bias_kernel, prefix_len, stretch_part, c...  0.75 us
  transfers between devices with their start and end apart: 5, of which 3 were waited for; matrix products, arithmetic and copies ran while one was open for 1% of the time, Pallas kernels for 11%

profile of v9, /device:TPU:15, one launch (start us, length us, event | category | flops | bytes accessed | tf_op | source)
XLA Modules:
  0.0 15.4 jit_solution(3003440281291297201)
XLA Ops:
  0.0 0.0 copy-start
  0.0 1.0 %shard_map.65 = (bf16[64,1024]{1,0:T(8,128)(2,1)S(1)}, bf16[256,512]{1,0:T(8,128)(2,1)S(1)}, bf16[256,512]{1,0:T(8,128)(2,1)S(1)}) custom-call(bf16[64,512]{1,0:T(8,128)(2,1)} %k_ref.1, bf16[64,512]{1,0:T(8,128)(2,1)} %v_ref.1, bf16[192,512]{1,0:T(8,128)(2,1)} %ck_ref.1, bf16[192,512]{1,0:T(8,128)(2,1)} %cv_ref.1), custom_call_target="tpu_custom_call" | custom-call | tf_op jit(solution)/shard_map/pallas_call | solution.py:242
  1.0 0.7 %collective-permute-start = (bf16[256,512]{1,0:T(8,128)(2,1)S(1)}, bf16[256,512]{1,0:T(8,128)(2,1)S(1)}, u32[]{:S(2)}, u32[]{:S(2)}) collective-permute-start(bf16[256,512]{1,0:T(8,128)(2,1)S(1)} %get-tuple-element.13), channel_id=1, source_target_pairs={{0,1},{1,0},{2,3},{3,2},{4,5},{5,4},{6,7},{7,6},{8,9},{9,8},{10,11... | collective-permute-start | bytes 786440 | tf_op jit(solution)/shard_map/ppermute | solution.py:20
  1.7 1.3 %collective-permute-start.1 = (bf16[64,1024]{1,0:T(8,128)(2,1)S(1)}, bf16[64,1024]{1,0:T(8,128)(2,1)S(1)}, u32[]{:S(2)}, u32[]{:S(2)}) collective-permute-start(bf16[64,1024]{1,0:T(8,128)(2,1)S(1)} %get-tuple-element.14), channel_id=1, source_target_pairs={{0,4},{4,8},{8,12},{12,0},{1,5},{5,9},{9,13},{13,1},{2,6},{6,10},{... | collective-permute-start | bytes 393224 | tf_op jit(solution)/shard_map/ppermute | solution.py:262
  3.0 0.0 collective-permute-done.peer_ref
  3.1 0.1 fusion
  3.1 4.1 %collective-permute-start.3 = (bf16[128,512]{1,0:T(8,128)(2,1)S(1)}, bf16[128,512]{1,0:T(8,128)(2,1)S(1)}, u32[]{:S(2)}, u32[]{:S(2)}) collective-permute-start(bf16[128,512]{1,0:T(8,128)(2,1)S(1)} %get-tuple-element.19), channel_id=1, source_target_pairs={{12,0},{13,1},{0,8},{5,13},{14,2},{15,3},{2,10},{7,15},{28,16},{29... | collective-permute-start | bytes 393224 | tf_op jit(solution)/shard_map/ppermute | solution.py:281
  7.2 1.3 %collective-permute-start.4 = (bf16[128,512]{1,0:T(8,128)(2,1)S(1)}, bf16[128,512]{1,0:T(8,128)(2,1)S(1)}, u32[]{:S(2)}, u32[]{:S(2)}) collective-permute-start(bf16[128,512]{1,0:T(8,128)(2,1)S(1)} %get-tuple-element.20), channel_id=1, source_target_pairs={{12,4},{13,5},{1,9},{4,12},{14,6},{15,7},{3,11},{6,14},{28,20},{29... | collective-permute-start | bytes 393224 | tf_op jit(solution)/shard_map/ppermute | solution.py:281
  8.5 0.0 collective-permute-done.1.near_ref
  8.6 1.7 %collective-permute-start.2 = (bf16[64,512]{1,0:T(8,128)(2,1)S(1)}, bf16[64,512]{1,0:T(8,128)(2,1)S(1)}, u32[]{:S(2)}, u32[]{:S(2)}) collective-permute-start(bf16[64,512]{1,0:T(8,128)(2,1)S(1)} %pad_maximum_fusion.1), channel_id=1, source_target_pairs={{0,1},{1,0},{2,3},{3,2},{4,5},{5,4},{6,7},{7,6},{8,9},{9,8},{10,11... | collective-permute-start | bytes 196616 | tf_op jit(solution)/shard_map/ppermute | solution.py:20
  10.3 0.0 copy-done
  10.3 0.8 %shard_map.64.bias_ref = f32[128,384]{1,0:T(8,128)S(1)} custom-call(s32[12]{0:T(128)} %len_ref.1), custom_call_target="tpu_custom_call" | custom-call | tf_op jit(solution)/shard_map/pallas_call | solution.py:252
  11.1 0.1 collective-permute-done.2.far_ref
  11.2 0.9 %shard_map.66 = (f32[128,2048]{1,0:T(8,128)S(1)}, f32[128,2048]{1,0:T(8,128)S(1)}, f32[128,2048]{1,0:T(8,128)S(1)}) custom-call(bf16[128,2048]{1,0:T(8,128)(2,1)S(1)} %constant_dynamic-slice_fusion.2.q_ref, f32[128,384]{1,0:T(8,128)S(1)} %shard_map.64.bias_ref, bf16[256,512]{1,0:T(8,128)(2,1)S(1)} %get-tuple-element.12.own_ref, ...), custom_call_target="tpu_custom_call" | custom-call | tf_op jit(solution)/shard_map/pallas_call | solution.py:300
  12.1 0.3 %collective-permute-done.3.refs_0_ = bf16[128,512]{1,0:T(8,128)(2,1)S(1)} collective-permute-done((bf16[128,512]{1,0:T(8,128)(2,1)S(1)}, bf16[128,512]{1,0:T(8,128)(2,1)S(1)}, u32[]{:S(2)}, u32[]{:S(2)}) %collective-permute-start.3) | collective-permute-done | bytes 131104 | tf_op jit(solution)/shard_map/ppermute | solution.py:281
  12.4 1.5 %collective-permute-done.4.refs_1_ = bf16[128,512]{1,0:T(8,128)(2,1)S(1)} collective-permute-done((bf16[128,512]{1,0:T(8,128)(2,1)S(1)}, bf16[128,512]{1,0:T(8,128)(2,1)S(1)}, u32[]{:S(2)}, u32[]{:S(2)}) %collective-permute-start.4) | collective-permute-done | bytes 131104 | tf_op jit(solution)/shard_map/ppermute | solution.py:281
  13.9 1.5 %shard_map.67 = bf16[128,2048]{1,0:T(8,128)(2,1)} custom-call(bf16[128,2048]{1,0:T(8,128)(2,1)S(1)} %constant_dynamic-slice_fusion.2.q_ref, f32[128,384]{1,0:T(8,128)S(1)} %shard_map.64.bias_ref, f32[128,2048]{1,0:T(8,128)S(1)} %get-tuple-element.16.max_ref, f32[128,2048]{1,0:T(8,128)S(1)} %get-tuple-element.17.sum_ref, ...), custom_call_target="tpu_custom_call" | custom-call | tf_op jit(solution)/shard_map/pallas_call | solution.py:307
  (5 shorter events, 0.1 us)
Async XLA Ops:
  0.0 10.3 %copy-start = (bf16[128,4096]{1,0:T(8,128)(2,1)S(1)}, bf16[128,4096]{1,0:T(8,128)(2,1)}, u32[]{:S(2)}) copy-start(bf16[128,4096]{1,0:T(8,128)(2,1)} %param.6) | copy-start | bytes 3145732
  1.0 2.0 %collective-permute-start = (bf16[256,512]{1,0:T(8,128)(2,1)S(1)}, bf16[256,512]{1,0:T(8,128)(2,1)S(1)}, u32[]{:S(2)}, u32[]{:S(2)}) collective-permute-start(bf16[256,512]{1,0:T(8,128)(2,1)S(1)} %get-tuple-element.13), channel_id=1, source_target_pairs={{0,1},{1,0},{2,3},{3,2},{4,5},{5,4},{6,7},{7,6},{8,9},{9,8},{10,11... | collective-permute-start | bytes 786440 | tf_op jit(solution)/shard_map/ppermute | solution.py:20
  1.7 6.8 %collective-permute-start.1 = (bf16[64,1024]{1,0:T(8,128)(2,1)S(1)}, bf16[64,1024]{1,0:T(8,128)(2,1)S(1)}, u32[]{:S(2)}, u32[]{:S(2)}) collective-permute-start(bf16[64,1024]{1,0:T(8,128)(2,1)S(1)} %get-tuple-element.14), channel_id=1, source_target_pairs={{0,4},{4,8},{8,12},{12,0},{1,5},{5,9},{9,13},{13,1},{2,6},{6,10},{... | collective-permute-start | bytes 393224 | tf_op jit(solution)/shard_map/ppermute | solution.py:262
  3.1 9.3 %collective-permute-start.3 = (bf16[128,512]{1,0:T(8,128)(2,1)S(1)}, bf16[128,512]{1,0:T(8,128)(2,1)S(1)}, u32[]{:S(2)}, u32[]{:S(2)}) collective-permute-start(bf16[128,512]{1,0:T(8,128)(2,1)S(1)} %get-tuple-element.19), channel_id=1, source_target_pairs={{12,0},{13,1},{0,8},{5,13},{14,2},{15,3},{2,10},{7,15},{28,16},{29... | collective-permute-start | bytes 393224 | tf_op jit(solution)/shard_map/ppermute | solution.py:281
  7.2 6.6 %collective-permute-start.4 = (bf16[128,512]{1,0:T(8,128)(2,1)S(1)}, bf16[128,512]{1,0:T(8,128)(2,1)S(1)}, u32[]{:S(2)}, u32[]{:S(2)}) collective-permute-start(bf16[128,512]{1,0:T(8,128)(2,1)S(1)} %get-tuple-element.20), channel_id=1, source_target_pairs={{12,4},{13,5},{1,9},{4,12},{14,6},{15,7},{3,11},{6,14},{28,20},{29... | collective-permute-start | bytes 393224 | tf_op jit(solution)/shard_map/ppermute | solution.py:281
  8.6 2.6 %collective-permute-start.2 = (bf16[64,512]{1,0:T(8,128)(2,1)S(1)}, bf16[64,512]{1,0:T(8,128)(2,1)S(1)}, u32[]{:S(2)}, u32[]{:S(2)}) collective-permute-start(bf16[64,512]{1,0:T(8,128)(2,1)S(1)} %pad_maximum_fusion.1), channel_id=1, source_target_pairs={{0,1},{1,0},{2,3},{3,2},{4,5},{5,4},{6,7},{7,6},{8,9},{9,8},{10,11... | collective-permute-start | bytes 196616 | tf_op jit(solution)/shard_map/ppermute | solution.py:20
